TPU v7x, 128 devices: a whole 4x4x4 slice. The times are simulated.
128 devices in a mesh: dp: 4 (over x), seq: 32 (over z, y, core).
Axes of the slice: x: 4, y: 4, z: 4, core: 2. Of those that a mesh axis runs over, the one named last changes fastest.
Arguments:
- inputs: bfloat16 [4, 4096, 960], P('dp', 'seq'), may hold values from -6 to 6
- w_project: bfloat16 [2, 960, 1600], P(None, 'dp', 'seq'), may hold values from -0.1875 to 0.1875
- w_output: bfloat16 [2, 960, 960], P(None, 'dp', 'seq'), may hold values from -1.5 to 1.5
- w_expand: bfloat16 [2, 960, 5120], P(None, 'dp', 'seq'), may hold values from -0.1875 to 0.1875
- w_contract: bfloat16 [2, 2560, 960], P(None, 'dp', 'seq'), may hold values from -0.125 to 0.125
- norm_gains: bfloat16 [3840], P(('dp', 'seq')), may hold values from 0.5 to 1.5
- segments: int32 [4, 4096], P('dp', 'seq'), may hold values from 0 to 20, as said below
- cotangent: bfloat16 [4, 4096, 960], P('dp', 'seq'), may hold values from -6 to 6
Outputs:
- block_output: bfloat16 [4, 4096, 960], P('dp', 'seq')
- input_gradient: float32 [4, 4096, 960], P('dp', 'seq')
- project_gradient: float32 [2, 960, 1600], P(None, 'dp', 'seq')
- output_gradient: float32 [2, 960, 960], P(None, 'dp', 'seq')
- expand_gradient: float32 [2, 960, 5120], P(None, 'dp', 'seq')
- contract_gradient: float32 [2, 2560, 960], P(None, 'dp', 'seq')
- gains_gradient: float32 [3840], P(('dp', 'seq'))
Inputs may be any that keep to these rules, and one draw needn't show every extreme that they name: `segments`: in each sequence the documents are numbered 0, 1, 2, ... in order of position, none empty. In one sequence of each draw, document 0 ends within the first 128 positions, document 1 runs to within the last 128 positions and document 2 fills the rest. In the sequence after it (cyclically) every document has max(200, 2) positions, except the last, which is cut at the sequence's end. In every other sequence the documents have max(200, 2) to 2000 positions each, except the last, which is cut at the sequence's end.
All inputs are finite; a program needn't handle non-finite values.
Results may differ from a plain program's by a relative error of at most 0.03.
Values may be sent and summed in bfloat16 or wider, within the bound.
No kernel may reach another device: no remote copies, remote signals or barrier semaphores. Data moves between devices by JAX's collectives and lax.ppermute only.
A program may use at most 192 MiB of HBM per device.

v0:
```python
import functools
import math

import jax
import jax.numpy as jnp
from jax import lax
from jax.experimental import pallas as pl
from jax.experimental.pallas import tpu as pltpu
from jax.sharding import PartitionSpec as P

HEADS = 15
KV_HEADS = 5
HEAD = 64
GROUP = HEADS // KV_HEADS
KVD = KV_HEADS * HEAD
WIDTH = 960
FF = 2560

EPSILON = 1e-05
THETA = 100000.0
MASKED = -1e30

RING_Y = [[z * 8 + y * 2 + c for y in range(4)] for z in range(4) for c in range(2)]
PLANE = [[i * 2 + c for i in range(16)] for c in range(2)]
SWAP = [(i, i ^ 1) for i in range(32)]

PADDED = 1024
EXPAND = 320
CONTRACT = 160
OUTPUT = 64
PROJECT = 128
LEAD = 144
GRADS = EXPAND + CONTRACT + OUTPUT
CHUNK = 512
LIMIT = 40 << 20

F32 = jnp.float32
BF16 = jnp.bfloat16
IN_VMEM = pl.BlockSpec(memory_space=pltpu.VMEM)
IN_SMEM = pl.BlockSpec(memory_space=pltpu.SMEM)


def shape(dims, dtype):
    return jax.ShapeDtypeStruct(dims, dtype)


def params():
    return pltpu.CompilerParams(vmem_limit_bytes=LIMIT)


def cost(flops, traffic):
    return pl.CostEstimate(flops=flops, bytes_accessed=traffic, transcendentals=0)


def nn_dot(left, right):
    return jnp.dot(left, right, preferred_element_type=F32)


def nt_dot(left, right):
    return lax.dot_general(left, right, (((1,), (1,)), ((), ())), preferred_element_type=F32)


def tn_dot(left, right):
    return lax.dot_general(left, right, (((0,), (0,)), ((), ())), preferred_element_type=F32)


def frequencies(size):
    half = size // 2
    return 1.0 / THETA ** (jnp.arange(half, dtype=F32) * 2.0 / size)


def norm_scale(stream):
    return lax.rsqrt(jnp.sum(stream * stream, axis=1, keepdims=True) / WIDTH + EPSILON)


def norm_pull(stream, gain, grad):
    scale = norm_scale(stream)
    weighted = gain * grad
    mean = jnp.sum(weighted * stream, axis=1, keepdims=True) / WIDTH
    grad_stream = scale * weighted - stream * (scale * scale * scale * mean)
    return grad_stream, jnp.sum(grad * stream * scale, axis=0, keepdims=True)


def tiles(ref, devices, start, rows, count, first):
    pieces = []
    for dp in range(ref.shape[0]):
        for tile in range(count):
            at = first + tile * rows
            block = ref[dp, start : start + devices, at : at + rows, :]
            pieces.append(block.reshape(devices * rows, 128))
    return jnp.concatenate(pieces, axis=1)


def project_specs(layer):
    if layer == 0:
        return [
            pl.BlockSpec((32, 4, 64, 128), lambda j: (0, 0, 0, 0)),
            pl.BlockSpec((32, 4, 64, 128), lambda j: (0, 0, 1, 0)),
        ]
    first = 2 * GRADS // 64
    return [
        pl.BlockSpec((4, 32, 64, 128), lambda j: (0, 0, first, 0)),
        pl.BlockSpec((4, 32, 64, 128), lambda j: (0, 0, first + 1, 0)),
    ]


def project_tiles(pair, start):
    pieces = []
    for dp in range(4):
        for ref in pair:
            if ref.shape[0] == 32:
                block = ref[start : start + 8, dp]
            else:
                block = ref[dp, start : start + 8]
            pieces.append(block.reshape(512, 128))
    return jnp.concatenate(pieces, axis=1)


def project_kernel(stream_ref, gain_ref, weight_one, weight_two, cosine_ref, sine_ref, *rest):
    query_ref, packed_ref, normed_ref, natural = rest
    stream = stream_ref[...]
    normed = (stream * norm_scale(stream) * gain_ref[...]).astype(BF16)
    normed_ref[...] = normed
    for part in range(4):
        result = nt_dot(project_tiles((weight_one, weight_two), part * 8), normed)
        for s in range(8):
            at = part * 8 + s
            natural[at * 50 : at * 50 + 50, :] = result[s * 64 : s * 64 + 50, :]
    cosine, sine = cosine_ref[...], sine_ref[...]
    for head in range(HEADS + KV_HEADS):
        at = head * HEAD
        first = natural[at : at + 32, :]
        second = natural[at + 32 : at + 64, :]
        one = first * cosine - second * sine
        two = second * cosine + first * sine
        if head < HEADS:
            both = jnp.concatenate([one, two], axis=0) * (1.0 / math.sqrt(HEAD))
            query_ref[at : at + 64, :] = both.astype(BF16)
        else:
            natural[at : at + 32, :] = one
            natural[at + 32 : at + 64, :] = two
    packed_ref[...] = natural[WIDTH : WIDTH + 2 * KVD, :].T.astype(BF16)


def project_forward(stream, gain, weight, layer, cosine, sine):
    tok = stream.shape[0]
    return pl.pallas_call(
        project_kernel,
        grid=(1,),
        out_shape=(
            shape((WIDTH, tok), BF16),
            shape((tok, 2 * KVD), BF16),
            shape((tok, PADDED), BF16),
        ),
        in_specs=[whole((tok, PADDED)), whole((1, PADDED))]
        + project_specs(layer)
        + [whole((32, tok)), whole((32, tok))],
        out_specs=(whole((WIDTH, tok)), whole((tok, 2 * KVD)), whole((tok, PADDED))),
        scratch_shapes=[pltpu.VMEM((WIDTH + 2 * KVD, tok), F32)],
        compiler_params=params(),
        cost_estimate=cost(2 * tok * 2048 * 1024, 5 << 20),
    )(stream, gain, weight, weight, cosine, sine)


def take_heads(ref, head):
    return jnp.concatenate(
        [ref[(GROUP * head + g) * HEAD : (GROUP * head + g + 1) * HEAD, :] for g in range(GROUP)],
        axis=1,
    )


def take_row(ref, head):
    return jnp.concatenate(
        [ref[GROUP * head + g : GROUP * head + g + 1, :] for g in range(GROUP)], axis=1
    )


def forward_kernel(
    range_ref, query_ref, packed_ref, bias_ref, mixed_ref, total_ref, top, total, mixed
):
    tok = query_ref.shape[1]
    top[...] = jnp.full(top.shape, MASKED, F32)
    total[...] = jnp.zeros(total.shape, F32)
    mixed[...] = jnp.zeros(mixed.shape, F32)

    def step(index, carry):
        rows = pl.ds(pl.multiple_of(index * CHUNK, CHUNK), CHUNK)
        bias = jnp.concatenate([bias_ref[rows, :]] * GROUP, axis=1)

        def scores_of(head):
            key = packed_ref[rows, head * HEAD : (head + 1) * HEAD]
            return nn_dot(key, take_heads(query_ref, head)) + bias

        later = scores_of(0)
        for head in range(KV_HEADS):
            scores = later
            if head + 1 < KV_HEADS:
                later = scores_of(head + 1)
            value = packed_ref[rows, KVD + head * HEAD : KVD + (head + 1) * HEAD]
            old_top = top[head]
            new_top = jnp.maximum(old_top, jnp.max(scores, axis=0, keepdims=True))
            raised = jnp.exp(scores - new_top)
            shrink = jnp.exp(old_top - new_top)
            top[head] = new_top
            total[head] = total[head] * shrink + jnp.sum(raised, axis=0, keepdims=True)
            mixed[head] = mixed[head] * shrink + tn_dot(value, raised.astype(BF16))
        return carry

    lax.fori_loop(range_ref[0], range_ref[1], step, 0)
    for head in range(KV_HEADS):
        result = mixed[head] / total[head]
        log_total = top[head] + jnp.log(total[head])
        for g in range(GROUP):
            at = GROUP * head + g
            columns = slice(g * tok, (g + 1) * tok)
            mixed_ref[at * HEAD : (at + 1) * HEAD, :] = result[:, columns]
            total_ref[at : at + 1, :] = log_total[:, columns]


def attend_forward(queries, packed, bias, chunk_range):
    tok = queries.shape[1]
    return pl.pallas_call(
        forward_kernel,
        out_shape=(shape((WIDTH, tok), F32), shape((HEADS, tok), F32)),
        in_specs=[IN_SMEM] + [IN_VMEM] * 3,
        out_specs=(IN_VMEM, IN_VMEM),
        scratch_shapes=[
            pltpu.VMEM((KV_HEADS, 1, GROUP * tok), F32),
            pltpu.VMEM((KV_HEADS, 1, GROUP * tok), F32),
            pltpu.VMEM((KV_HEADS, HEAD, GROUP * tok), F32),
        ],
        compiler_params=params(),
        cost_estimate=cost(4 * 4096 * 128 * 960, 8 << 20),
    )(chunk_range, queries, packed, bias)


def backward_kernel(
    range_ref,
    query_ref,
    packed_ref,
    bias_ref,
    total_ref,
    inner_ref,
    grad_ref,
    query_out,
    packed_out,
    grad_query,
):
    tok = query_ref.shape[1]
    packed_out[...] = jnp.zeros(packed_out.shape, packed_out.dtype)
    grad_query[...] = jnp.zeros(grad_query.shape, F32)

    def step(index, carry):
        rows = pl.ds(pl.multiple_of(index * CHUNK, CHUNK), CHUNK)
        bias = jnp.concatenate([bias_ref[rows, :]] * GROUP, axis=1)

        def products(head):
            key = packed_ref[rows, head * HEAD : (head + 1) * HEAD]
            value = packed_ref[rows, KVD + head * HEAD : KVD + (head + 1) * HEAD]
            scores = nn_dot(key, take_heads(query_ref, head)) + bias
            return key, scores, nn_dot(value, take_heads(grad_ref, head))

        later = products(0)
        for head in range(KV_HEADS):
            key, scores, grad_chance = later
            if head + 1 < KV_HEADS:
                later = products(head + 1)
            chance = jnp.exp(scores - take_row(total_ref, head))
            grad_scores = (chance * (grad_chance - take_row(inner_ref, head))).astype(BF16)
            grad_key = nt_dot(grad_scores, take_heads(query_ref, head)).astype(BF16)
            grad_value = nt_dot(chance.astype(BF16), take_heads(grad_ref, head)).astype(BF16)
            key_lanes = slice(head * HEAD, (head + 1) * HEAD)
            value_lanes = slice(KVD + head * HEAD, KVD + (head + 1) * HEAD)
            for block in range(CHUNK // tok):
                at = index * (CHUNK // tok // 2) + block // 2
                part = slice(block * tok, (block + 1) * tok)
                packed_out[block % 2, at, :, key_lanes] = grad_key[part, :]
                packed_out[block % 2, at, :, value_lanes] = grad_value[part, :]
            grad_query[head] += tn_dot(key, grad_scores)
        return carry

    lax.fori_loop(range_ref[0], range_ref[1], step, 0)
    for head in range(KV_HEADS):
        result = grad_query[head] * (1.0 / math.sqrt(HEAD))
        for g in range(GROUP):
            at = GROUP * head + g
            query_out[at * HEAD : (at + 1) * HEAD, :] = result[:, g * tok : (g + 1) * tok]


def attend_backward(queries, packed, bias, chunk_range, log_total, inner, grad_mixed):
    tok = queries.shape[1]
    return pl.pallas_call(
        backward_kernel,
        out_shape=(shape((WIDTH, tok), F32), shape((2, 16, tok, 2 * KVD), BF16)),
        in_specs=[IN_SMEM] + [IN_VMEM] * 6,
        out_specs=(IN_VMEM, IN_VMEM),
        scratch_shapes=[pltpu.VMEM((KV_HEADS, HEAD, GROUP * tok), F32)],
        compiler_params=params(),
        cost_estimate=cost(10 * 4096 * 128 * 960, 13 << 20),
    )(chunk_range, queries, packed, bias, log_total, inner, grad_mixed)


def feed_kernel(
    stream_ref, mixed_ref, gain_ref, output_ref, gate_w, up_w, contract_w, *rest
):
    mixed_out, middle_out, normed_out, gate_out, up_out, hidden_out, stream_out = rest
    tok = stream_ref.shape[0]

    @pl.when(pl.program_id(0) == 0)
    def _():
        pieces = []
        for dp in range(4):
            pieces += [mixed_ref[dp * 240 : dp * 240 + 240, :], jnp.zeros((16, tok), F32)]
        mixed = jnp.concatenate(pieces, axis=0).T.astype(BF16)
        mixed_out[...] = mixed
        middle = stream_ref[...] + nt_dot(mixed, tiles(output_ref, 32, 0, 32, 2, 0))
        middle_out[...] = middle
        normed_out[...] = (middle * norm_scale(middle) * gain_ref[...]).astype(BF16)
        stream_out[...] = middle

    normed = normed_out[...]
    gate = nt_dot(normed, tiles(gate_w, 4, 0, 160, 2, 0))
    up = nt_dot(normed, tiles(up_w, 4, 0, 160, 2, 0))
    gate_out[...] = gate
    up_out[...] = up
    hidden = (gate / (1.0 + jnp.exp(-gate)) * up).astype(BF16)
    hidden_out[...] = hidden
    stream_out[...] += nt_dot(hidden, tiles(contract_w, 32, 0, 32, 5, 0))


def whole(dims):
    return pl.BlockSpec(dims, lambda j: (0,) * len(dims))


def weight_specs(layer):
    return [
        pl.BlockSpec((4, 32, OUTPUT, 128), lambda j: (0, 0, 15 + layer, 0)),
        pl.BlockSpec((4, 4, EXPAND, 128), lambda j: (0, j, layer, 0)),
        pl.BlockSpec((4, 4, EXPAND, 128), lambda j: (0, j + 4, layer, 0)),
        pl.BlockSpec((1, 32, CONTRACT, 128), lambda j: (j, 0, 4 + layer, 0)),
    ]


def feed_forward(stream, mixed, gain, bulk, layer):
    tok = stream.shape[0]
    column = pl.BlockSpec((tok, 640), lambda j: (0, j))
    return pl.pallas_call(
        feed_kernel,
        grid=(4,),
        out_shape=(
            shape((tok, PADDED), BF16),
            shape((tok, PADDED), F32),
            shape((tok, PADDED), BF16),
            shape((tok, FF), F32),
            shape((tok, FF), F32),
            shape((tok, FF), BF16),
            shape((tok, PADDED), F32),
        ),
        in_specs=[whole((tok, PADDED)), whole((WIDTH, tok)), whole((1, PADDED))]
        + weight_specs(layer),
        out_specs=(whole((tok, PADDED)),) * 3 + (column,) * 3 + (whole((tok, PADDED)),),
        compiler_params=params(),
        cost_estimate=cost(2 * tok * 9000 * 1024, 18 << 20),
    )(stream, mixed, gain, bulk, bulk, bulk, bulk)


def feed_pull_kernel(
    grad_ref,
    middle_ref,
    gain_ref,
    mixed_ref,
    gate_ref,
    up_ref,
    output_ref,
    gate_w,
    up_w,
    contract_w,
    *rest,
):
    low_out, gate_up_out, middle_out, middle_low_out, gain_out, mixed_out, inner_out, total = rest
    index = pl.program_id(0)
    tok = grad_ref.shape[0]

    @pl.when(index == 0)
    def _():
        low_out[...] = grad_ref[...].astype(BF16)
        total[...] = jnp.zeros_like(total)

    gate, up = gate_ref[...], up_ref[...]
    grad_hidden = nn_dot(low_out[...], tiles(contract_w, 32, 0, 32, 5, 0))
    chance = 1.0 / (1.0 + jnp.exp(-gate))
    swish = gate * chance
    grad_gate = (grad_hidden * up * (chance + swish * (1.0 - chance))).astype(BF16)
    grad_up = (grad_hidden * swish).astype(BF16)
    gate_up_out[0] = grad_gate
    gate_up_out[1] = grad_up
    total[...] += nn_dot(grad_gate, tiles(gate_w, 4, 0, 160, 2, 0)) + nn_dot(
        grad_up, tiles(up_w, 4, 0, 160, 2, 0)
    )

    @pl.when(index == pl.num_programs(0) - 1)
    def _():
        grad_part, grad_gain = norm_pull(middle_ref[...], gain_ref[...], total[...])
        grad_middle = grad_ref[...] + grad_part
        middle_out[...] = grad_middle
        gain_out[...] = grad_gain
        low = grad_middle.astype(BF16)
        middle_low_out[...] = low
        back = nn_dot(low, tiles(output_ref, 32, 0, 32, 2, 0)).astype(BF16).astype(F32).T
        for dp in range(4):
            mixed_out[dp * 240 : dp * 240 + 240, :] = back[dp * 256 : dp * 256 + 240, :].astype(BF16)
        for head in range(HEADS):
            rows = slice(head * HEAD, head * HEAD + HEAD)
            product = mixed_out[rows, :].astype(F32) * mixed_ref[rows, :]
            inner_out[head : head + 1, :] = jnp.sum(product, axis=0, keepdims=True)


def feed_backward(grad, middle, gain, mixed, gate, up, bulk, layer):
    tok = grad.shape[0]
    column = pl.BlockSpec((tok, 640), lambda j: (0, j))
    return pl.pallas_call(
        feed_pull_kernel,
        grid=(4,),
        out_shape=(
            shape((tok, PADDED), BF16),
            shape((2, tok, FF), BF16),
            shape((tok, PADDED), F32),
            shape((tok, PADDED), BF16),
            shape((1, PADDED), F32),
            shape((WIDTH, tok), BF16),
            shape((HEADS, tok), F32),
        ),
        in_specs=[
            whole((tok, PADDED)),
            whole((tok, PADDED)),
            whole((1, PADDED)),
            whole((WIDTH, tok)),
            column,
            column,
        ]
        + weight_specs(layer),
        out_specs=(
            whole((tok, PADDED)),
            pl.BlockSpec((2, tok, 640), lambda j: (0, 0, j)),
            whole((tok, PADDED)),
            whole((tok, PADDED)),
            whole((1, PADDED)),
            whole((WIDTH, tok)),
            whole((HEADS, tok)),
        ),
        scratch_shapes=[pltpu.VMEM((tok, PADDED), F32)],
        compiler_params=params(),
        cost_estimate=cost(2 * tok * 9000 * 1024, 18 << 20),
    )(grad, middle, gain, mixed, gate, up, bulk, bulk, bulk, bulk)


def put_tiles(out_ref, result, rows, count, first):
    for dp in range(4):
        for tile in range(count):
            at = (dp * count + tile) * 128
            block = result[:, at : at + 128].reshape(4, rows, 128).astype(BF16)
            out_ref[:, dp, first + tile * rows : first + (tile + 1) * rows, :] = block


def weight_kernel(with_project, *refs):
    gate_ref, normed_ref, low_ref, hidden_ref, middle_ref, mixed_ref = refs[:6]
    out_ref = refs[-1]
    put_tiles(out_ref, tn_dot(gate_ref[0], normed_ref[...]), 160, 2, 0)
    put_tiles(out_ref, tn_dot(low_ref[...], hidden_ref[...]), 32, 5, EXPAND)
    put_tiles(out_ref, tn_dot(middle_ref[...], mixed_ref[...]), 32, 2, EXPAND + CONTRACT)
    if with_project:
        put_tiles(out_ref, nn_dot(refs[6][...], refs[7][...]), 64, 2, GRADS)


def weight_gradients(grad_gate_up, normed_feed, grad_low, hidden, middle_low, mixed, project):
    tok = normed_feed.shape[0]
    rows = GRADS + (PROJECT if project else 0)
    operands = [grad_gate_up, normed_feed, grad_low, hidden, middle_low, mixed]
    in_specs = [
        pl.BlockSpec((1, tok, 640), lambda j: (j // 4, 0, j % 4)),
        whole((tok, PADDED)),
        pl.BlockSpec((tok, 128), lambda j: (0, j)),
        whole((tok, FF)),
        pl.BlockSpec((tok, 128), lambda j: (0, j)),
        whole((tok, PADDED)),
    ]
    if project:
        operands += list(project)
        in_specs += [pl.BlockSpec((256, tok), lambda j: (j, 0)), whole((tok, PADDED))]
    return pl.pallas_call(
        functools.partial(weight_kernel, bool(project)),
        grid=(8,),
        out_shape=shape((32, 4, rows, 128), BF16),
        in_specs=in_specs,
        out_specs=pl.BlockSpec((4, 4, rows, 128), lambda j: (j, 0, 0, 0)),
        compiler_params=params(),
        cost_estimate=cost(2 * tok * 11000 * 1024, 20 << 20),
    )(*operands)


def project_pull_kernel(
    query_ref,
    local_ref,
    cosine_ref,
    sine_ref,
    weight_one,
    weight_two,
    stream_ref,
    gain_ref,
    grad_ref,
    *rest,
):
    padded_out, grad_out, gain_out, natural, spread = rest
    tok = stream_ref.shape[0]
    natural[0:WIDTH, :] = query_ref[...]
    natural[WIDTH : WIDTH + 2 * KVD, :] = local_ref[...].T
    cosine, sine = cosine_ref[...], sine_ref[...]
    for head in range(HEADS + KV_HEADS):
        at = head * HEAD
        first = natural[at : at + 32, :]
        second = natural[at + 32 : at + 64, :]
        natural[at : at + 32, :] = first * cosine + second * sine
        natural[at + 32 : at + 64, :] = second * cosine - first * sine
    for s in range(32):
        spread[s * 64 : s * 64 + 50, :] = natural[s * 50 : s * 50 + 50, :]
        spread[s * 64 + 50 : s * 64 + 64, :] = jnp.zeros((14, tok), F32)
    total = jnp.zeros((tok, PADDED), F32)
    for part in range(4):
        block = spread[part * 512 : (part + 1) * 512, :].astype(BF16)
        padded_out[part * 512 : (part + 1) * 512, :] = block
        total = total + tn_dot(block, project_tiles((weight_one, weight_two), part * 8))
    grad_part, grad_gain = norm_pull(stream_ref[...], gain_ref[...], total)
    grad_out[...] = grad_ref[...] + grad_part
    gain_out[...] = grad_gain


def project_backward(grad_query, grad_local, cosine, sine, weight, layer, stream, gain, grad_middle):
    tok = stream.shape[0]
    return pl.pallas_call(
        project_pull_kernel,
        grid=(1,),
        out_shape=(
            shape((2048, tok), BF16),
            shape((tok, PADDED), F32),
            shape((1, PADDED), F32),
        ),
        in_specs=[
            whole((WIDTH, tok)),
            whole((tok, 2 * KVD)),
            whole((32, tok)),
            whole((32, tok)),
        ]
        + project_specs(layer)
        + [whole((tok, PADDED)), whole((1, PADDED)), whole((tok, PADDED))],
        out_specs=(whole((2048, tok)), whole((tok, PADDED)), whole((1, PADDED))),
        scratch_shapes=[
            pltpu.VMEM((WIDTH + 2 * KVD, tok), F32),
            pltpu.VMEM((2048, tok), F32),
        ],
        compiler_params=params(),
        cost_estimate=cost(2 * tok * 2048 * 1024, 6 << 20),
    )(grad_query, grad_local, cosine, sine, weight, weight, stream, gain, grad_middle)


def lead_kernel(padded_ref, normed_ref, gains_ref, out_ref):
    result = nn_dot(padded_ref[...], normed_ref[...])
    for dp in range(4):
        for tile in range(2):
            at = (dp * 2 + tile) * 128
            block = result[:, at : at + 128].reshape(2, 2, 64, 128).astype(BF16)
            for core in range(2):
                out_ref[core, :, dp, tile * 64 : tile * 64 + 64, :] = block[:, core]
    for core in range(2):
        for place in range(2):
            out_ref[core, place, :, PROJECT:LEAD, :] = gains_ref[place * 2 + core]


def lead_gradients(padded, normed, gains):
    tok = normed.shape[0]
    return pl.pallas_call(
        lead_kernel,
        grid=(8,),
        out_shape=shape((2, 16, 4, LEAD, 128), BF16),
        in_specs=[
            pl.BlockSpec((256, tok), lambda j: (j, 0)),
            whole((tok, PADDED)),
            pl.BlockSpec((4, 4, LEAD - PROJECT, 128), lambda j: (j, 0, 0, 0)),
        ],
        out_specs=pl.BlockSpec((2, 2, 4, LEAD, 128), lambda j: (0, j, 0, 0, 0)),
        compiler_params=params(),
        cost_estimate=cost(2 * tok * 2048 * 1024, 6 << 20),
    )(padded, normed, gains)


def swap_cores(array):
    return lax.ppermute(array, "seq", SWAP)


def hop_y(array, hop):
    moves = [(i, i // 8 * 8 + (i % 8 + 2 * hop) % 8) for i in range(32)]
    return lax.ppermute(array, "seq", moves)


def hop_z(array, hop):
    return lax.ppermute(array, "seq", [(i, (i + 8 * hop) % 32) for i in range(32)])


def ring(array, move):
    return jnp.stack([array] + [move(array, hop) for hop in (1, 2, 3)])


def order_kernel(place_ref, first_own, last_own, first_other, last_other, out_ref):
    for s in range(32):
        back_z = lax.rem(place_ref[0] - s // 8 + 4, 4)
        back_y = lax.rem(place_ref[1] - s // 2 % 4 + 4, 4)
        same = place_ref[2] == s % 2

        @pl.when(same)
        def _(s=s, back_z=back_z, back_y=back_y):
            out_ref[s, 0] = first_own[back_z, back_y]
            out_ref[s, 1] = last_own[back_y, back_z]

        @pl.when(jnp.logical_not(same))
        def _(s=s, back_z=back_z, back_y=back_y):
            out_ref[s, 0] = first_other[back_z, back_y]
            out_ref[s, 1] = last_other[back_y, back_z]


def gather_seq(array):
    index = lax.axis_index("seq")
    first = ring(array[0], hop_y)
    last = ring(array[1], hop_z)
    first = ring(first, hop_z)
    last = ring(last, hop_y)
    place = jnp.stack([index // 8, index // 2 % 4, index % 2]).astype(jnp.int32)
    return pl.pallas_call(
        order_kernel,
        out_shape=shape((32,) + array.shape, array.dtype),
        in_specs=[IN_SMEM] + [IN_VMEM] * 4,
        out_specs=IN_VMEM,
        compiler_params=params(),
        cost_estimate=cost(0, 12 << 20),
    )(place, first, last, swap_cores(first), swap_cores(last))


def reduce_seq(array):
    core = lax.axis_index("seq") % 2
    mine = lax.dynamic_index_in_dim(array, core, 0, keepdims=False)
    theirs = lax.dynamic_index_in_dim(array, 1 - core, 0, keepdims=False)
    arrived = swap_cores(theirs)
    both = (mine.astype(F32) + arrived.astype(F32)).astype(BF16)
    spread = lax.all_to_all(both, "seq", 0, 0, axis_index_groups=PLANE, tiled=True)
    return jnp.sum(spread.astype(F32), axis=0)


def reduce_dp(array):
    array = array.astype(BF16)
    place = lax.axis_index("dp")
    total = lax.dynamic_index_in_dim(array, place, 0, keepdims=False).astype(F32)
    for hop in (1, 2, 3):
        block = lax.dynamic_index_in_dim(array, (place + hop) % 4, 0, keepdims=False)
        moved = lax.ppermute(block, "dp", [(i, (i + hop) % 4) for i in range(4)])
        total = total + moved.astype(F32)
    return total


def pad_last(array, size):
    return jnp.pad(array, [(0, 0)] * (array.ndim - 1) + [(0, size - array.shape[-1])])


def pad_groups(array):
    groups = array.reshape(array.shape[:-1] + (array.shape[-1] // 30, 30))
    return pad_last(groups, 32).reshape(array.shape[:-1] + (-1,))


def drop_groups(array):
    groups = array.reshape(array.shape[:-1] + (array.shape[-1] // 32, 32))
    return groups[..., :30].reshape(array.shape[:-1] + (-1,))


def to_tiles(array, rows):
    array = jnp.pad(array, ((0, rows - array.shape[0]), (0, 0)))
    count = array.shape[1] // 128
    return array.reshape(rows, count, 128).transpose(1, 0, 2).reshape(count * rows, 128)


def from_tiles(array, rows):
    count = array.shape[0] // rows
    return array.reshape(count, rows, 128).transpose(1, 0, 2).reshape(rows, count * 128)


def on_device(inputs, w_project, w_output, w_expand, w_contract, norm_gains, segments, cotangent):
    tok = inputs.shape[1]
    layers = 2
    local_segment = segments[0]

    pieces = [to_tiles(pad_groups(w_expand[layer].T), 160) for layer in range(layers)]
    pieces += [to_tiles(w_contract[layer].T, 32) for layer in range(layers)]
    pieces += [to_tiles(pad_last(w_output[layer].T, 256), 32) for layer in range(layers)]
    pieces += [to_tiles(pad_groups(w_project[1].T), 64)]
    bulk = lax.all_gather(jnp.concatenate(pieces, axis=0), ("dp", "seq"))
    bulk = bulk.reshape((4, 32) + bulk.shape[1:])

    extra = jnp.zeros((LEAD - PROJECT - 2, 128), BF16)
    lead = jnp.concatenate(
        [
            to_tiles(pad_groups(w_project[0].T), 64),
            pad_last(norm_gains[None, :], 128),
            local_segment.astype(BF16)[None, :],
            extra,
        ],
        axis=0,
    )
    leads = lax.all_gather(lead, "dp").reshape(2, 2, LEAD, 128)
    leads = gather_seq(leads).reshape(32, 4, LEAD, 128)
    gains = leads[:, :, PROJECT, :32].transpose(1, 0, 2).reshape(4, 1, PADDED).astype(F32)
    all_segment = lax.dynamic_index_in_dim(
        leads[:, :, PROJECT + 1, :], lax.axis_index("dp"), 1, keepdims=False
    )
    all_segment = all_segment.reshape(-1).astype(jnp.int32)
    length = all_segment.shape[0]
    projects = [leads, bulk]

    query_index = lax.axis_index("seq") * tok + jnp.arange(tok, dtype=jnp.int32)
    key_index = jnp.arange(length, dtype=jnp.int32)
    starts = jnp.sum((all_segment[:, None] < local_segment[None, :]).astype(jnp.int32), axis=0)
    position = (query_index - starts).astype(F32)
    angle = frequencies(HEAD)[:, None] * position[None, :]
    cosine = jnp.cos(angle)
    sine = jnp.sin(angle)
    allowed = (local_segment[None, :] == all_segment[:, None]) & (
        query_index[None, :] >= key_index[:, None]
    )
    bias = jnp.where(allowed, 0.0, MASKED).astype(F32)
    chunk_range = jnp.stack([starts[0] // CHUNK, query_index[-1] // CHUNK + 1])

    stream = pad_groups(inputs[0]).astype(F32)
    records = []
    for layer in range(layers):
        queries, packed_local, normed = project_forward(
            stream, gains[2 * layer], projects[layer], layer, cosine, sine
        )
        packed = gather_seq(packed_local.reshape(2, tok // 2, 2 * KVD)).reshape(length, 2 * KVD)
        mixed_wide, log_total = attend_forward(queries, packed, bias, chunk_range)
        mixed, middle, normed_feed, gate, up, hidden, after = feed_forward(
            stream, mixed_wide, gains[2 * layer + 1], bulk, layer
        )
        records.append(
            (stream, queries, packed, normed, mixed_wide, log_total)
            + (mixed, middle, normed_feed, gate, up, hidden)
        )
        stream = after
    block_output = drop_groups(stream.astype(BF16))[None]

    grad_stream = pad_groups(cotangent[0]).astype(F32)
    gain_grads = [None] * 4
    bulk_grads = [None] * layers
    project = None
    for layer in reversed(range(layers)):
        stream_in, queries, packed, normed, mixed_wide, log_total = records[layer][:6]
        mixed, middle, normed_feed, gate, up, hidden = records[layer][6:]
        grad_low, grad_gate_up, grad_middle, middle_low, gain_grad, grad_mixed, inner = (
            feed_backward(
                grad_stream, middle, gains[2 * layer + 1], mixed_wide, gate, up, bulk, layer
            )
        )
        gain_grads[2 * layer + 1] = gain_grad
        payload = weight_gradients(
            grad_gate_up, normed_feed, grad_low, hidden, middle_low, mixed, project
        )
        bulk_grads[layer] = lax.psum_scatter(payload, "seq", scatter_dimension=0)
        grad_query, grad_packed = attend_backward(
            queries, packed, bias, chunk_range, log_total, inner, grad_mixed
        )
        grad_local = reduce_seq(grad_packed)
        padded, grad_stream, gain_grad = project_backward(
            grad_query,
            grad_local,
            cosine,
            sine,
            projects[layer],
            layer,
            stream_in,
            gains[2 * layer],
            grad_middle,
        )
        gain_grads[2 * layer] = gain_grad
        project = (padded, normed)

    gain_rows = jnp.concatenate(gain_grads, axis=0).astype(BF16).reshape(4, 32, 32)
    gain_rows = gain_rows.transpose(1, 0, 2)[:, :, None, :]
    gain_rows = jnp.pad(gain_rows, ((0, 0), (0, 0), (0, LEAD - PROJECT - 1), (0, 96)))
    second = reduce_dp(bulk_grads[1])
    lead_grads, second = lax.optimization_barrier(
        (lead_gradients(padded, normed, gain_rows), second)
    )
    lead_part = reduce_dp(reduce_seq(lead_grads))
    first = reduce_dp(bulk_grads[0])
    parts = [first, second]
    last_part = first[GRADS:]

    def project_out(tile_rows):
        return drop_groups(from_tiles(tile_rows, 64)[:50]).T

    expand_out = jnp.stack([drop_groups(from_tiles(part[:EXPAND], 160)).T for part in parts])
    contract_out = jnp.stack(
        [from_tiles(part[EXPAND : EXPAND + CONTRACT], 32)[:30].T for part in parts]
    )
    output_out = jnp.stack(
        [from_tiles(part[EXPAND + CONTRACT : GRADS], 32)[:30, :240].T for part in parts]
    )
    return (
        block_output,
        drop_groups(grad_stream)[None],
        jnp.stack([project_out(lead_part[:PROJECT]), project_out(last_part)]),
        output_out,
        expand_out,
        contract_out,
        lead_part[PROJECT, :30],
    )


def solution(mesh):
    in_specs = (
        P("dp", "seq", None),
        P(None, "dp", "seq"),
        P(None, "dp", "seq"),
        P(None, "dp", "seq"),
        P(None, "dp", "seq"),
        P(("dp", "seq")),
        P("dp", "seq"),
        P("dp", "seq", None),
    )
    out_specs = (
        P("dp", "seq", None),
        P("dp", "seq", None),
        P(None, "dp", "seq"),
        P(None, "dp", "seq"),
        P(None, "dp", "seq"),
        P(None, "dp", "seq"),
        P(("dp", "seq")),
    )
    return jax.shard_map(
        on_device, mesh=mesh, in_specs=in_specs, out_specs=out_specs, check_vma=False
    )
```

profile of v0, /device:TPU:1, one launch (start us, length us, event | category | flops | bytes accessed | tf_op | source)
XLA Modules:
  0.0 646.0 jit_solution(14493573849225078510)
XLA Ops:
  12.0 10.3 %all-gather = bf16[576,128]{1,0:T(8,128)(2,1)S(1)} all-gather(bf16[144,128]{1,0:T(8,128)(2,1)S(1)} %fusion.15), channel_id=2, replica_groups=mesh['dp'=4,'seq'=32] {'dp'}, dimensions={0}, use_global_device_ids=true | all-gather | bytes 184320 | tf_op jit(solution)/shard_map/all_gather | solution.py:714
  26.7 4.1 collective-permute-done.1
  45.2 6.7 %collective-permute-done.3 = bf16[4,2,144,128]{3,2,1,0:T(8,128)(2,1)S(1)} collective-permute-done((bf16[4,2,144,128]{3,2,1,0:T(8,128)(2,1)S(1)}, bf16[4,2,144,128]{3,2,1,0:T(8,128)(2,1)S(1)}, u32[]{:S(2)}, u32[]{:S(2)}) %collective-permute-start.3) | collective-permute-done | bytes 294944 | tf_op jit(solution)/shard_map/ppermute | solution.py:605
  52.1 16.4 %collective-permute-start.12 = (bf16[4,4,2,144,128]{4,3,2,1,0:T(8,128)(2,1)S(1)}, bf16[4,4,2,144,128]{4,3,2,1,0:T(8,128)(2,1)}, u32[]{:S(2)}, u32[]{:S(2)}) collective-permute-start(bf16[4,4,2,144,128]{4,3,2,1,0:T(8,128)(2,1)S(1)} %pad_maximum_fusion.4.first_own), channel_id=1, source_target_pairs={{0,1},{1,0},{2,3},{3,2},{4,5},{5,4},{6,7},{7,6},{8,9},{9,8},{10,11... | collective-permute-start | bytes 3538952 | tf_op jit(solution)/shard_map/ppermute | solution.py:596
  68.7 5.1 collective-permute-start.13
  90.4 4.5 collective-permute-done.16
  99.1 3.8 collective-permute-start.19
  107.9 12.4 %collective-permute-done.22 = bf16[64,640]{1,0:T(8,128)(2,1)S(1)} collective-permute-done((bf16[64,640]{1,0:T(8,128)(2,1)S(1)}, bf16[64,640]{1,0:T(8,128)(2,1)S(1)}, u32[]{:S(2)}, u32[]{:S(2)}) %collective-permute-start.22) | collective-permute-done | bytes 81952 | tf_op jit(solution)/shard_map/ppermute | solution.py:605
  127.6 13.4 %collective-permute-done.17 = bf16[4,64,640]{2,1,0:T(8,128)(2,1)S(1)} collective-permute-done((bf16[4,64,640]{2,1,0:T(8,128)(2,1)S(1)}, bf16[4,64,640]{2,1,0:T(8,128)(2,1)S(1)}, u32[]{:S(2)}, u32[]{:S(2)}) %collective-permute-start.17) | collective-permute-done | bytes 327712 | tf_op jit(solution)/shard_map/ppermute | solution.py:605
  144.5 6.5 %collective-permute-done.23 = bf16[4,64,640]{2,1,0:T(8,128)(2,1)S(1)} collective-permute-done((bf16[4,64,640]{2,1,0:T(8,128)(2,1)S(1)}, bf16[4,64,640]{2,1,0:T(8,128)(2,1)S(1)}, u32[]{:S(2)}, u32[]{:S(2)}) %collective-permute-start.23) | collective-permute-done | bytes 327712 | tf_op jit(solution)/shard_map/ppermute | solution.py:601
  152.3 3.9 collective-permute-start.27
  170.6 10.3 %shard_map.139 = (bf16[128,1024]{1,0:T(8,128)(2,1)S(1)}, f32[128,1024]{1,0:T(8,128)S(1)}, bf16[128,1024]{1,0:T(8,128)(2,1)S(1)}, f32[128,2560]{1,0:T(8,128)S(1)}...) custom-call(f32[128,1024]{1,0:T(8,128)S(1)} %copy.85.stream_ref, ...), custom_call_target="tpu_custom_call" | custom-call | flops 2359296000 | bytes 18874368 | tf_op jit(solution)/shard_map/pallas_call | solution.py:347
  182.1 4.8 shard_map.140
  198.3 6.1 collective-permute-start.33
  214.2 8.5 %collective-permute-start.38 = (bf16[4,64,640]{2,1,0:T(8,128)(2,1)S(1)}, bf16[4,64,640]{2,1,0:T(8,128)(2,1)S(1)}, u32[]{:S(2)}, u32[]{:S(2)}) collective-permute-start(bf16[4,64,640]{2,1,0:T(8,128)(2,1)S(1)} %get-tuple-element.132), channel_id=1, source_target_pairs={{0,4},{1,5},{2,6},{3,7},{4,0},{5,1},{6,2},{7,3},{8,12},{9,13},{10,... | collective-permute-start | bytes 983048 | tf_op jit(solution)/shard_map/ppermute | solution.py:601
  225.0 7.9 %collective-permute-start.40 = (bf16[4,4,64,640]{3,2,1,0:T(8,128)(2,1)}, bf16[4,4,64,640]{3,2,1,0:T(8,128)(2,1)}, u32[]{:S(2)}, u32[]{:S(2)}) collective-permute-start(bf16[4,4,64,640]{3,2,1,0:T(8,128)(2,1)} %pad_maximum_fusion.2.first_own), channel_id=1, source_target_pairs={{0,1},{1,0},{2,3},{3,2},{4,5},{5,4},{6,7},{7,6},{8,9},{9,8},{10,11... | collective-permute-start | bytes 3932168 | tf_op jit(solution)/shard_map/ppermute | solution.py:596
  251.3 10.4 %shard_map.143 = (bf16[128,1024]{1,0:T(8,128)(2,1)S(1)}, f32[128,1024]{1,0:T(8,128)S(1)}, bf16[128,1024]{1,0:T(8,128)(2,1)S(1)}, f32[128,2560]{1,0:T(8,128)S(1)}...) custom-call(f32[128,1024]{1,0:T(8,128)S(1)} %get-tuple-element.60.stream_ref, ...), custom_call_target="tpu_custom_call" | custom-call | flops 2359296000 | bytes 18874368 | tf_op jit(solution)/shard_map/pallas_call | solution.py:347
  262.6 9.2 %shard_map.144 = (bf16[128,1024]{1,0:T(8,128)(2,1)S(1)}, bf16[2,128,2560]{2,1,0:T(8,128)(2,1)S(1)}, f32[128,1024]{1,0:T(8,128)S(1)}, bf16[128,1024]{1,0:T(8,128)...) custom-call(f32[128,1024]{1,0:T(8,128)S(1)} %copy-done.8, ...), custom_call_target="tpu_custom_call" | custom-call | flops 2359296000 | bytes 18874368 | tf_op jit(solution)/shard_map/pallas_call | solution.py:421
  273.2 9.7 %shard_map.151 = bf16[32,4,544,128]{3,2,1,0:T(8,128)(2,1)} custom-call(bf16[2,128,2560]{2,1,0:T(8,128)(2,1)S(1)} %get-tuple-element.91.refs_0_, bf16[128,1024]{1,0:T(8,128)(2,1)S(1)} %get-tuple-element.92.refs_1_, bf16[128,1024]{1,0:T(8,128)(2,1)S(1)} %get-tuple-element.93.refs_2_, bf16[128,2560]{1,0:T(8,128)(2,1)S(1)} %get-tuple-element.94.refs_3_, ...), custom_call_target="tpu_custom_call" | custom-call | flops 2883584000 | bytes 20971520 | tf_op jit(solution)/shard_map/pallas_call | solution.py:490
  295.1 5.2 collective-permute-done.42
  303.7 53.2 %all_to_all.15 = bf16[16,128,640]{2,1,0:T(8,128)(2,1)S(1)} all-to-all(bf16[16,128,640]{2,1,0:T(8,128)(2,1)S(1)} %fusion.1), channel_id=1, replica_groups={{0,2,4,6,8,10,12,14,16,18,20,22,24,26,28,30},{1,3,5,7,9,11,13,15,17,19,..., dimensions={0} | all-to-all | bytes 5242880 | tf_op jit(solution)/shard_map/all_to_all | solution.py:652
  361.6 9.4 %shard_map.147 = (bf16[128,1024]{1,0:T(8,128)(2,1)S(1)}, bf16[2,128,2560]{2,1,0:T(8,128)(2,1)S(1)}, f32[128,1024]{1,0:T(8,128)S(1)}, bf16[128,1024]{1,0:T(8,128)...) custom-call(f32[128,1024]{1,0:T(8,128)S(1)} %get-tuple-element.75.grad_ref, ...), custom_call_target="tpu_custom_call" | custom-call | flops 2359296000 | bytes 18874368 | tf_op jit(solution)/shard_map/pallas_call | solution.py:421
  371.7 11.0 %shard_map.152 = bf16[32,4,672,128]{3,2,1,0:T(8,128)(2,1)} custom-call(bf16[2,128,2560]{2,1,0:T(8,128)(2,1)S(1)} %get-tuple-element.98.refs_0_, bf16[128,1024]{1,0:T(8,128)(2,1)S(1)} %copy-done.29, bf16[128,1024]{1,0:T(8,128)(2,1)S(1)} %get-tuple-element.100.refs_2_, bf16[128,2560]{1,0:T(8,128)(2,1)S(1)} %copy-done.17, ...), custom_call_target="tpu_custom_call" | custom-call | flops 2883584000 | bytes 20971520 | tf_op jit(solution)/shard_map/pallas_call | solution.py:490
  394.1 4.5 collective-permute-done.43
  401.0 9.9 %all-to-all-start.1 = ((bf16[16,128,640]{2,1,0:T(8,128)(2,1)}), bf16[16,128,640]{2,1,0:T(8,128)(2,1)}, u32[]{:S(2)}, u32[]{:S(2)}) async-start(bf16[16,128,640]{2,1,0:T(8,128)(2,1)} %fusion), calls=%async_computation.1 | async-start | bytes 5242880 | tf_op jit(solution)/shard_map/all_to_all | solution.py:652
  411.2 43.2 %all-to-all-done.1 = bf16[16,128,640]{2,1,0:T(8,128)(2,1)} async-done(((bf16[16,128,640]{2,1,0:T(8,128)(2,1)}), bf16[16,128,640]{2,1,0:T(8,128)(2,1)}, u32[]{:S(2)}, u32[]{:S(2)}) %all-to-all-start.1) | async-done | bytes 2621472 | tf_op jit(solution)/shard_map/all_to_all | solution.py:652
  461.6 55.6 %collective-permute-start.45 = (bf16[544,128]{1,0:T(8,128)(2,1)S(1)}, bf16[544,128]{1,0:T(8,128)(2,1)S(1)}, u32[]{:S(2)}, u32[]{:S(2)}) collective-permute-start(bf16[544,128]{1,0:T(8,128)(2,1)S(1)} %get-tuple-element.130), channel_id=1, source_target_pairs={{0,64},{32,96},{64,0},{96,32},{1,65},{33,97},{65,1},{97,33},{2,66}... | collective-permute-start | bytes 417800 | tf_op jit(solution)/shard_map/ppermute | solution.py:662
  526.7 4.2 collective-permute-done.47
  532.9 4.6 all-to-all-start.2
  539.5 50.2 %all-to-all-done.2 = bf16[16,4,144,128]{3,2,1,0:T(8,128)(2,1)} async-done(((bf16[16,4,144,128]{3,2,1,0:T(8,128)(2,1)}), bf16[16,4,144,128]{3,2,1,0:T(8,128)(2,1)}, u32[]{:S(2)}, u32[]{:S(2)}) %all-to-all-start.2) | async-done | bytes 2359328 | tf_op jit(solution)/shard_map/all_to_all | solution.py:652
  598.9 20.8 %reduce-scatter.5.cloned.1.call-done = bf16[1,4,672,128]{3,2,1,0:T(8,128)(2,1)} async-done(((bf16[32,4,672,128]{3,2,1,0:T(8,128)(2,1)}), bf16[1,4,672,128]{3,2,1,0:T(8,128)(2,1)}) %reduce-scatter.5.cloned.1.call-update) | async-done | bytes 688144 | tf_op jit(solution)/shard_map/reduce_scatter | solution.py:771
  629.0 5.2 collective-permute-done.51
  (367 shorter events, 196.6 us)
Async XLA Ops:
  7.2 162.4 %all-gather.4.cloned.1.call-start = ((), (), s32[]{:S(2)}) async-start(), calls=%async_computation.7 | async-start | bytes 40157184 | tf_op jit(solution)/shard_map/all_gather | solution.py:701
  11.5 449.0 %reduce-scatter.3.cloned.1.call-start = ((), (), s32[]{:S(2)}) async-start(), calls=%async_computation.5 | async-start | bytes 18382848 | tf_op jit(solution)/shard_map/reduce_scatter | solution.py:771
  32.1 12.4 %collective-permute-start.5 = (bf16[4,2,144,128]{3,2,1,0:T(8,128)(2,1)S(1)}, bf16[4,2,144,128]{3,2,1,0:T(8,128)(2,1)S(1)}, u32[]{:S(2)}, u32[]{:S(2)}) collective-permute-start(bf16[4,2,144,128]{3,2,1,0:T(8,128)(2,1)S(1)} %get-tuple-element.142), channel_id=1, source_target_pairs={{0,24},{1,25},{2,26},{3,27},{4,28},{5,29},{6,30},{7,31},{8,0},{9,1... | collective-permute-start | bytes 884744 | tf_op jit(solution)/shard_map/ppermute | solution.py:605
  41.3 10.7 %collective-permute-start.3 = (bf16[4,2,144,128]{3,2,1,0:T(8,128)(2,1)S(1)}, bf16[4,2,144,128]{3,2,1,0:T(8,128)(2,1)S(1)}, u32[]{:S(2)}, u32[]{:S(2)}) collective-permute-start(bf16[4,2,144,128]{3,2,1,0:T(8,128)(2,1)S(1)} %get-tuple-element.142), channel_id=1, source_target_pairs={{0,8},{1,9},{2,10},{3,11},{4,12},{5,13},{6,14},{7,15},{8,16},{9,17... | collective-permute-start | bytes 884744 | tf_op jit(solution)/shard_map/ppermute | solution.py:605
  41.6 27.0 %collective-permute-start.11 = (bf16[4,2,144,128]{3,2,1,0:T(8,128)(2,1)S(1)}, bf16[4,2,144,128]{3,2,1,0:T(8,128)(2,1)S(1)}, u32[]{:S(2)}, u32[]{:S(2)}) collective-permute-start(bf16[4,2,144,128]{3,2,1,0:T(8,128)(2,1)S(1)} %get-tuple-element.140), channel_id=1, source_target_pairs={{0,6},{1,7},{2,0},{3,1},{4,2},{5,3},{6,4},{7,5},{8,14},{9,15},{10,... | collective-permute-start | bytes 884744 | tf_op jit(solution)/shard_map/ppermute | solution.py:601
  43.9 24.6 %collective-permute-start.10 = (bf16[4,2,144,128]{3,2,1,0:T(8,128)(2,1)S(1)}, bf16[4,2,144,128]{3,2,1,0:T(8,128)(2,1)S(1)}, u32[]{:S(2)}, u32[]{:S(2)}) collective-permute-start(bf16[4,2,144,128]{3,2,1,0:T(8,128)(2,1)S(1)} %get-tuple-element.140), channel_id=1, source_target_pairs={{0,4},{1,5},{2,6},{3,7},{4,0},{5,1},{6,2},{7,3},{8,12},{9,13},{10,... | collective-permute-start | bytes 884744 | tf_op jit(solution)/shard_map/ppermute | solution.py:601
  44.6 24.0 %collective-permute-start.9 = (bf16[4,2,144,128]{3,2,1,0:T(8,128)(2,1)S(1)}, bf16[4,2,144,128]{3,2,1,0:T(8,128)(2,1)S(1)}, u32[]{:S(2)}, u32[]{:S(2)}) collective-permute-start(bf16[4,2,144,128]{3,2,1,0:T(8,128)(2,1)S(1)} %get-tuple-element.140), channel_id=1, source_target_pairs={{0,2},{1,3},{2,4},{3,5},{4,6},{5,7},{6,0},{7,1},{8,10},{9,11},{10,... | collective-permute-start | bytes 884744 | tf_op jit(solution)/shard_map/ppermute | solution.py:601
  52.1 22.2 %collective-permute-start.12 = (bf16[4,4,2,144,128]{4,3,2,1,0:T(8,128)(2,1)S(1)}, bf16[4,4,2,144,128]{4,3,2,1,0:T(8,128)(2,1)}, u32[]{:S(2)}, u32[]{:S(2)}) collective-permute-start(bf16[4,4,2,144,128]{4,3,2,1,0:T(8,128)(2,1)S(1)} %pad_maximum_fusion.4.first_own), channel_id=1, source_target_pairs={{0,1},{1,0},{2,3},{3,2},{4,5},{5,4},{6,7},{7,6},{8,9},{9,8},{10,11... | collective-permute-start | bytes 3538952 | tf_op jit(solution)/shard_map/ppermute | solution.py:596
  90.0 9.0 %collective-permute-start.14 = (bf16[64,640]{1,0:T(8,128)(2,1)S(1)}, bf16[64,640]{1,0:T(8,128)(2,1)S(1)}, u32[]{:S(2)}, u32[]{:S(2)}) collective-permute-start(bf16[64,640]{1,0:T(8,128)(2,1)S(1)} %get-tuple-element.152), channel_id=1, source_target_pairs={{0,2},{1,3},{2,4},{3,5},{4,6},{5,7},{6,0},{7,1},{8,10},{9,11},{10,... | collective-permute-start | bytes 245768 | tf_op jit(solution)/shard_map/ppermute | solution.py:601
  99.1 24.8 %collective-permute-start.19 = (bf16[4,64,640]{2,1,0:T(8,128)(2,1)S(1)}, bf16[4,64,640]{2,1,0:T(8,128)(2,1)S(1)}, u32[]{:S(2)}, u32[]{:S(2)}) collective-permute-start(bf16[4,64,640]{2,1,0:T(8,128)(2,1)S(1)} %get-tuple-element.138), channel_id=1, source_target_pairs={{0,24},{1,25},{2,26},{3,27},{4,28},{5,29},{6,30},{7,31},{8,0},{9,1... | collective-permute-start | bytes 983048 | tf_op jit(solution)/shard_map/ppermute | solution.py:605
  102.9 17.4 %collective-permute-start.22 = (bf16[64,640]{1,0:T(8,128)(2,1)S(1)}, bf16[64,640]{1,0:T(8,128)(2,1)S(1)}, u32[]{:S(2)}, u32[]{:S(2)}) collective-permute-start(bf16[64,640]{1,0:T(8,128)(2,1)S(1)} %get-tuple-element.151), channel_id=1, source_target_pairs={{0,24},{1,25},{2,26},{3,27},{4,28},{5,29},{6,30},{7,31},{8,0},{9,1... | collective-permute-start | bytes 245768 | tf_op jit(solution)/shard_map/ppermute | solution.py:605
  103.0 18.3 %collective-permute-start.21 = (bf16[64,640]{1,0:T(8,128)(2,1)S(1)}, bf16[64,640]{1,0:T(8,128)(2,1)S(1)}, u32[]{:S(2)}, u32[]{:S(2)}) collective-permute-start(bf16[64,640]{1,0:T(8,128)(2,1)S(1)} %get-tuple-element.151), channel_id=1, source_target_pairs={{0,16},{1,17},{2,18},{3,19},{4,20},{5,21},{6,22},{7,23},{8,24},{9,... | collective-permute-start | bytes 245768 | tf_op jit(solution)/shard_map/ppermute | solution.py:605
  103.2 18.0 %collective-permute-start.20 = (bf16[64,640]{1,0:T(8,128)(2,1)S(1)}, bf16[64,640]{1,0:T(8,128)(2,1)S(1)}, u32[]{:S(2)}, u32[]{:S(2)}) collective-permute-start(bf16[64,640]{1,0:T(8,128)(2,1)S(1)} %get-tuple-element.151), channel_id=1, source_target_pairs={{0,8},{1,9},{2,10},{3,11},{4,12},{5,13},{6,14},{7,15},{8,16},{9,17... | collective-permute-start | bytes 245768 | tf_op jit(solution)/shard_map/ppermute | solution.py:605
  104.3 23.3 %collective-permute-start.18 = (bf16[4,64,640]{2,1,0:T(8,128)(2,1)S(1)}, bf16[4,64,640]{2,1,0:T(8,128)(2,1)S(1)}, u32[]{:S(2)}, u32[]{:S(2)}) collective-permute-start(bf16[4,64,640]{2,1,0:T(8,128)(2,1)S(1)} %get-tuple-element.138), channel_id=1, source_target_pairs={{0,16},{1,17},{2,18},{3,19},{4,20},{5,21},{6,22},{7,23},{8,24},{9,... | collective-permute-start | bytes 983048 | tf_op jit(solution)/shard_map/ppermute | solution.py:605
  120.3 20.6 %collective-permute-start.17 = (bf16[4,64,640]{2,1,0:T(8,128)(2,1)S(1)}, bf16[4,64,640]{2,1,0:T(8,128)(2,1)S(1)}, u32[]{:S(2)}, u32[]{:S(2)}) collective-permute-start(bf16[4,64,640]{2,1,0:T(8,128)(2,1)S(1)} %get-tuple-element.138), channel_id=1, source_target_pairs={{0,8},{1,9},{2,10},{3,11},{4,12},{5,13},{6,14},{7,15},{8,16},{9,17... | collective-permute-start | bytes 983048 | tf_op jit(solution)/shard_map/ppermute | solution.py:605
  121.3 23.2 %collective-permute-start.25 = (bf16[4,64,640]{2,1,0:T(8,128)(2,1)S(1)}, bf16[4,64,640]{2,1,0:T(8,128)(2,1)S(1)}, u32[]{:S(2)}, u32[]{:S(2)}) collective-permute-start(bf16[4,64,640]{2,1,0:T(8,128)(2,1)S(1)} %get-tuple-element.136), channel_id=1, source_target_pairs={{0,6},{1,7},{2,0},{3,1},{4,2},{5,3},{6,4},{7,5},{8,14},{9,15},{10,... | collective-permute-start | bytes 983048 | tf_op jit(solution)/shard_map/ppermute | solution.py:601
  122.6 21.9 %collective-permute-start.24 = (bf16[4,64,640]{2,1,0:T(8,128)(2,1)S(1)}, bf16[4,64,640]{2,1,0:T(8,128)(2,1)S(1)}, u32[]{:S(2)}, u32[]{:S(2)}) collective-permute-start(bf16[4,64,640]{2,1,0:T(8,128)(2,1)S(1)} %get-tuple-element.136), channel_id=1, source_target_pairs={{0,4},{1,5},{2,6},{3,7},{4,0},{5,1},{6,2},{7,3},{8,12},{9,13},{10,... | collective-permute-start | bytes 983048 | tf_op jit(solution)/shard_map/ppermute | solution.py:601
  123.9 27.1 %collective-permute-start.23 = (bf16[4,64,640]{2,1,0:T(8,128)(2,1)S(1)}, bf16[4,64,640]{2,1,0:T(8,128)(2,1)S(1)}, u32[]{:S(2)}, u32[]{:S(2)}) collective-permute-start(bf16[4,64,640]{2,1,0:T(8,128)(2,1)S(1)} %get-tuple-element.136), channel_id=1, source_target_pairs={{0,2},{1,3},{2,4},{3,5},{4,6},{5,7},{6,0},{7,1},{8,10},{9,11},{10,... | collective-permute-start | bytes 983048 | tf_op jit(solution)/shard_map/ppermute | solution.py:601
  142.2 18.2 %collective-permute-start.26 = (bf16[4,4,64,640]{3,2,1,0:T(8,128)(2,1)}, bf16[4,4,64,640]{3,2,1,0:T(8,128)(2,1)}, u32[]{:S(2)}, u32[]{:S(2)}) collective-permute-start(bf16[4,4,64,640]{3,2,1,0:T(8,128)(2,1)} %pad_maximum_fusion.first_own), channel_id=1, source_target_pairs={{0,1},{1,0},{2,3},{3,2},{4,5},{5,4},{6,7},{7,6},{8,9},{9,8},{10,11... | collective-permute-start | bytes 3932168 | tf_op jit(solution)/shard_map/ppermute | solution.py:596
  198.3 24.4 %collective-permute-start.33 = (bf16[4,64,640]{2,1,0:T(8,128)(2,1)S(1)}, bf16[4,64,640]{2,1,0:T(8,128)(2,1)S(1)}, u32[]{:S(2)}, u32[]{:S(2)}) collective-permute-start(bf16[4,64,640]{2,1,0:T(8,128)(2,1)S(1)} %get-tuple-element.134), channel_id=1, source_target_pairs={{0,24},{1,25},{2,26},{3,27},{4,28},{5,29},{6,30},{7,31},{8,0},{9,1... | collective-permute-start | bytes 983048 | tf_op jit(solution)/shard_map/ppermute | solution.py:605
  206.6 16.1 %collective-permute-start.32 = (bf16[4,64,640]{2,1,0:T(8,128)(2,1)S(1)}, bf16[4,64,640]{2,1,0:T(8,128)(2,1)S(1)}, u32[]{:S(2)}, u32[]{:S(2)}) collective-permute-start(bf16[4,64,640]{2,1,0:T(8,128)(2,1)S(1)} %get-tuple-element.134), channel_id=1, source_target_pairs={{0,16},{1,17},{2,18},{3,19},{4,20},{5,21},{6,22},{7,23},{8,24},{9,... | collective-permute-start | bytes 983048 | tf_op jit(solution)/shard_map/ppermute | solution.py:605
  212.9 10.8 %collective-permute-start.31 = (bf16[4,64,640]{2,1,0:T(8,128)(2,1)S(1)}, bf16[4,64,640]{2,1,0:T(8,128)(2,1)S(1)}, u32[]{:S(2)}, u32[]{:S(2)}) collective-permute-start(bf16[4,64,640]{2,1,0:T(8,128)(2,1)S(1)} %get-tuple-element.134), channel_id=1, source_target_pairs={{0,8},{1,9},{2,10},{3,11},{4,12},{5,13},{6,14},{7,15},{8,16},{9,17... | collective-permute-start | bytes 983048 | tf_op jit(solution)/shard_map/ppermute | solution.py:605
  214.1 18.8 %collective-permute-start.39 = (bf16[4,64,640]{2,1,0:T(8,128)(2,1)S(1)}, bf16[4,64,640]{2,1,0:T(8,128)(2,1)S(1)}, u32[]{:S(2)}, u32[]{:S(2)}) collective-permute-start(bf16[4,64,640]{2,1,0:T(8,128)(2,1)S(1)} %get-tuple-element.132), channel_id=1, source_target_pairs={{0,6},{1,7},{2,0},{3,1},{4,2},{5,3},{6,4},{7,5},{8,14},{9,15},{10,... | collective-permute-start | bytes 983048 | tf_op jit(solution)/shard_map/ppermute | solution.py:601
  214.2 18.7 %collective-permute-start.38 = (bf16[4,64,640]{2,1,0:T(8,128)(2,1)S(1)}, bf16[4,64,640]{2,1,0:T(8,128)(2,1)S(1)}, u32[]{:S(2)}, u32[]{:S(2)}) collective-permute-start(bf16[4,64,640]{2,1,0:T(8,128)(2,1)S(1)} %get-tuple-element.132), channel_id=1, source_target_pairs={{0,4},{1,5},{2,6},{3,7},{4,0},{5,1},{6,2},{7,3},{8,12},{9,13},{10,... | collective-permute-start | bytes 983048 | tf_op jit(solution)/shard_map/ppermute | solution.py:601
  222.7 13.2 %collective-permute-start.37 = (bf16[4,64,640]{2,1,0:T(8,128)(2,1)S(1)}, bf16[4,64,640]{2,1,0:T(8,128)(2,1)S(1)}, u32[]{:S(2)}, u32[]{:S(2)}) collective-permute-start(bf16[4,64,640]{2,1,0:T(8,128)(2,1)S(1)} %get-tuple-element.132), channel_id=1, source_target_pairs={{0,2},{1,3},{2,4},{3,5},{4,6},{5,7},{6,0},{7,1},{8,10},{9,11},{10,... | collective-permute-start | bytes 983048 | tf_op jit(solution)/shard_map/ppermute | solution.py:601
  225.0 20.3 %collective-permute-start.40 = (bf16[4,4,64,640]{3,2,1,0:T(8,128)(2,1)}, bf16[4,4,64,640]{3,2,1,0:T(8,128)(2,1)}, u32[]{:S(2)}, u32[]{:S(2)}) collective-permute-start(bf16[4,4,64,640]{3,2,1,0:T(8,128)(2,1)} %pad_maximum_fusion.2.first_own), channel_id=1, source_target_pairs={{0,1},{1,0},{2,3},{3,2},{4,5},{5,4},{6,7},{7,6},{8,9},{9,8},{10,11... | collective-permute-start | bytes 3932168 | tf_op jit(solution)/shard_map/ppermute | solution.py:596
  282.9 336.8 %reduce-scatter.5.cloned.1.call-start = ((), (), s32[]{:S(2)}) async-start(), calls=%async_computation.6 | async-start | bytes 22708224 | tf_op jit(solution)/shard_map/reduce_scatter | solution.py:771
  401.0 53.4 %all-to-all-start.1 = ((bf16[16,128,640]{2,1,0:T(8,128)(2,1)}), bf16[16,128,640]{2,1,0:T(8,128)(2,1)}, u32[]{:S(2)}, u32[]{:S(2)}) async-start(bf16[16,128,640]{2,1,0:T(8,128)(2,1)} %fusion), calls=%async_computation.1 | async-start | bytes 5242880 | tf_op jit(solution)/shard_map/all_to_all | solution.py:652
  461.5 59.2 %collective-permute-start.46 = (bf16[544,128]{1,0:T(8,128)(2,1)S(1)}, bf16[544,128]{1,0:T(8,128)(2,1)S(1)}, u32[]{:S(2)}, u32[]{:S(2)}) collective-permute-start(bf16[544,128]{1,0:T(8,128)(2,1)S(1)} %get-tuple-element.129), channel_id=1, source_target_pairs={{0,96},{32,0},{64,32},{96,64},{1,97},{33,1},{65,33},{97,65},{2,98}... | collective-permute-start | bytes 417800 | tf_op jit(solution)/shard_map/ppermute | solution.py:662
  461.6 59.1 %collective-permute-start.45 = (bf16[544,128]{1,0:T(8,128)(2,1)S(1)}, bf16[544,128]{1,0:T(8,128)(2,1)S(1)}, u32[]{:S(2)}, u32[]{:S(2)}) collective-permute-start(bf16[544,128]{1,0:T(8,128)(2,1)S(1)} %get-tuple-element.130), channel_id=1, source_target_pairs={{0,64},{32,96},{64,0},{96,32},{1,65},{33,97},{65,1},{97,33},{2,66}... | collective-permute-start | bytes 417800 | tf_op jit(solution)/shard_map/ppermute | solution.py:662
  532.9 56.8 %all-to-all-start.2 = ((bf16[16,4,144,128]{3,2,1,0:T(8,128)(2,1)}), bf16[16,4,144,128]{3,2,1,0:T(8,128)(2,1)}, u32[]{:S(2)}, u32[]{:S(2)}) async-start(bf16[16,4,144,128]{3,2,1,0:T(8,128)(2,1)} %fusion.2), calls=%async_computation.3 | async-start | bytes 4718592 | tf_op jit(solution)/shard_map/all_to_all | solution.py:652
  623.9 10.4 %collective-permute-start.51 = (bf16[672,128]{1,0:T(8,128)(2,1)S(1)}, bf16[672,128]{1,0:T(8,128)(2,1)S(1)}, u32[]{:S(2)}, u32[]{:S(2)}) collective-permute-start(bf16[672,128]{1,0:T(8,128)(2,1)S(1)} %get-tuple-element.125), channel_id=1, source_target_pairs={{0,32},{32,64},{64,96},{96,0},{1,33},{33,65},{65,97},{97,1},{2,34}... | collective-permute-start | bytes 516104 | tf_op jit(solution)/shard_map/ppermute | solution.py:662
  (78 other events, 684.7 us)
Sparse Core Ops, SparseCore 0:
  11.6 150.4 all-gather.3
  283.0 175.4 reduce-scatter.2
  463.0 156.6 reduce-scatter.4
where the time goes:
time: 659 us; the launch traced here: 646 us
  waiting for transfers between devices  219 us (33%)
  starting transfers between devices  174 us (26%)
  Pallas kernels  95.3 us (14%)
  blocking collectives  63.5 us (10%)
  local copies, waits for them, and re-layouts  51.4 us (8%)
  other arithmetic  24.1 us (4%)
  between operations  18.4 us (3%)
    all_to_all x2, waiting for transfers between devices, reduce_seq(): lax.all_to_all(both, 'seq', 0, 0, axis_index_groups=PLANE, tiled=True)  93.3 us
    ppermute x9, starting transfers between devices, reduce_dp(): moved = lax.ppermute(block, 'dp', [(i, (i + hop) % 4) for i in range(4)])  62.5 us
    all_to_all x1, blocking collectives, reduce_seq(): lax.all_to_all(both, 'seq', 0, 0, axis_index_groups=PLANE, tiled=True)  53.2 us
    ppermute x18, waiting for transfers between devices, hop_z(): lax.ppermute(array, 'seq', [(i, (i + 8 * hop) % 32) for i in range(32)])  42.1 us
    ppermute x9, starting transfers between devices, swap_cores(): return lax.ppermute(array, 'seq', SWAP)  41.8 us
    unnamed x116, local copies, waits for them, and re-layouts  33 us
    ppermute x18, starting transfers between devices, hop_z(): lax.ppermute(array, 'seq', [(i, (i + 8 * hop) % 32) for i in range(32)])  30.2 us
    ppermute x18, waiting for transfers between devices, hop_y(): return lax.ppermute(array, 'seq', moves)  29.9 us
  transfers between devices with their start and end apart: 59, of which 33 were waited for; matrix products, arithmetic and copies ran while one was open for 6% of the time, Pallas kernels for 7%

commit v1 on v0

--- a/solution.py
+++ b/solution.py
@@ -653,6 +653,31 @@
     return jnp.sum(spread.astype(F32), axis=0)
 
 
+def ring_sum(array, place, move):
+    total = lax.dynamic_index_in_dim(array, place, 0, keepdims=False).astype(F32)
+    for hop in (1, 2, 3):
+        block = lax.dynamic_index_in_dim(array, (place + hop) % 4, 0, keepdims=False)
+        total = total + move(block, hop).astype(F32)
+    return total
+
+
+def reduce_packed(array):
+    index = lax.axis_index("seq")
+    core, along_y, along_z = index % 2, index // 2 % 4, index // 8
+    rows, width = array.shape[2] // 2, array.shape[3]
+    mine = lax.dynamic_index_in_dim(array, core, 0, keepdims=False)
+    theirs = lax.dynamic_index_in_dim(array, 1 - core, 0, keepdims=False)
+    both = mine.astype(F32) + swap_cores(theirs).astype(F32)
+    both = both.astype(BF16).reshape(4, 4, 2, rows, width)
+    first = both[:, :, 0]
+    last = both[:, :, 1].transpose(1, 0, 2, 3)
+    first = ring_sum(first, along_z, hop_z).astype(BF16)
+    last = ring_sum(last, along_y, hop_y).astype(BF16)
+    first = ring_sum(first, along_y, hop_y)
+    last = ring_sum(last, along_z, hop_z)
+    return jnp.concatenate([first, last], axis=0)
+
+
 def reduce_dp(array):
     array = array.astype(BF16)
     place = lax.axis_index("dp")
@@ -772,7 +797,7 @@
         grad_query, grad_packed = attend_backward(
             queries, packed, bias, chunk_range, log_total, inner, grad_mixed
         )
-        grad_local = reduce_seq(grad_packed)
+        grad_local = reduce_packed(grad_packed)
         padded, grad_stream, gain_grad = project_backward(
             grad_query,
             grad_local,

time: 659 us -> 645 us (0.979)
  blocking collectives: 63.5 us -> 10.3 us
  starting transfers between devices: 174 us -> 207 us
  local copies, waits for them, and re-layouts: 51.4 us -> 58 us
    all_to_all x1 -> x0, blocking collectives: 53.2 us -> none  [reduce_seq(): lax.all_to_all(both, 'seq', 0, 0, axis_index_groups=PLANE, tiled=True)]
    all_to_all x2 -> x1, waiting for transfers between devices: 93.3 us -> 49.3 us  [reduce_seq(): lax.all_to_all(both, 'seq', 0, 0, axis_index_groups=PLANE, tiled=True)]
    ppermute x18 -> x30, starting transfers between devices: 30.2 us -> 70.2 us  [hop_z(): lax.ppermute(array, 'seq', [(i, (i + 8 * hop) % 32) for i in range(32)])]
    ppermute x18 -> x30, waiting for transfers between devices: 29.9 us -> 56.5 us  [hop_y(): return lax.ppermute(array, 'seq', moves)]
    ppermute x18 -> x30, waiting for transfers between devices: 42.1 us -> 63.8 us  [hop_z(): lax.ppermute(array, 'seq', [(i, (i + 8 * hop) % 32) for i in range(32)])]
    convert_element_type x0 -> x6, other arithmetic: none -> 11 us  [the longest x2 6.63 us: reduce_packed(): both = both.astype(BF16).reshape(4, 4, 2, rows, width)]
    ppermute x18 -> x30, starting transfers between devices: 25.3 us -> 35.8 us  [hop_y(): return lax.ppermute(array, 'seq', moves)]
    all_to_all x2 -> x1, starting transfers between devices: 14.5 us -> 4.56 us  [reduce_seq(): lax.all_to_all(both, 'seq', 0, 0, axis_index_groups=PLANE, tiled=True)]
  transfers between devices with their start and end apart: 59 -> 82, of which waited for: 33 -> 43; matrix products, arithmetic and copies ran while one was open for 6% -> 7% of each run, Pallas kernels for 7% -> 7%
where the time goes in v1:
time: 645 us; the launch traced here: 635 us
  waiting for transfers between devices  218 us (34%)
  starting transfers between devices  207 us (32%)
  Pallas kernels  96 us (15%)
  local copies, waits for them, and re-layouts  58 us (9%)
  other arithmetic  27 us (4%)
  between operations  18.6 us (3%)
  blocking collectives  10.3 us (2%)
    ppermute x30, starting transfers between devices, hop_z(): lax.ppermute(array, 'seq', [(i, (i + 8 * hop) % 32) for i in range(32)])  70.2 us
    ppermute x30, waiting for transfers between devices, hop_z(): lax.ppermute(array, 'seq', [(i, (i + 8 * hop) % 32) for i in range(32)])  63.8 us
    ppermute x30, waiting for transfers between devices, hop_y(): return lax.ppermute(array, 'seq', moves)  56.5 us
    ppermute x9, starting transfers between devices, reduce_dp(): moved = lax.ppermute(block, 'dp', [(i, (i + hop) % 4) for i in range(4)])  55 us
    all_to_all x1, waiting for transfers between devices, reduce_seq(): lax.all_to_all(both, 'seq', 0, 0, axis_index_groups=PLANE, tiled=True)  49.3 us
    ppermute x9, starting transfers between devices, swap_cores(): return lax.ppermute(array, 'seq', SWAP)  41.2 us
    ppermute x30, starting transfers between devices, hop_y(): return lax.ppermute(array, 'seq', moves)  35.8 us
    unnamed x126, local copies, waits for them, and re-layouts  32.6 us
  transfers between devices with their start and end apart: 82, of which 43 were waited for; matrix products, arithmetic and copies ran while one was open for 7% of the time, Pallas kernels for 7%

profile of v1, /device:TPU:1, one launch (start us, length us, event | category | flops | bytes accessed | tf_op | source)
XLA Modules:
  0.0 635.1 jit_solution(9098819874936534162)
XLA Ops:
  12.0 10.3 %all-gather = bf16[576,128]{1,0:T(8,128)(2,1)S(1)} all-gather(bf16[144,128]{1,0:T(8,128)(2,1)S(1)} %fusion.35), channel_id=2, replica_groups=mesh['dp'=4,'seq'=32] {'dp'}, dimensions={0}, use_global_device_ids=true | all-gather | bytes 184320 | tf_op jit(solution)/shard_map/all_gather | solution.py:739
  45.2 6.8 %collective-permute-done.3 = bf16[4,2,144,128]{3,2,1,0:T(8,128)(2,1)S(1)} collective-permute-done((bf16[4,2,144,128]{3,2,1,0:T(8,128)(2,1)S(1)}, bf16[4,2,144,128]{3,2,1,0:T(8,128)(2,1)S(1)}, u32[]{:S(2)}, u32[]{:S(2)}) %collective-permute-start.3) | collective-permute-done | bytes 294944 | tf_op jit(solution)/shard_map/ppermute | solution.py:605
  52.2 16.3 %collective-permute-start.12 = (bf16[4,4,2,144,128]{4,3,2,1,0:T(8,128)(2,1)S(1)}, bf16[4,4,2,144,128]{4,3,2,1,0:T(8,128)(2,1)}, u32[]{:S(2)}, u32[]{:S(2)}) collective-permute-start(bf16[4,4,2,144,128]{4,3,2,1,0:T(8,128)(2,1)S(1)} %pad_maximum_fusion.4.first_own), channel_id=1, source_target_pairs={{0,1},{1,0},{2,3},{3,2},{4,5},{5,4},{6,7},{7,6},{8,9},{9,8},{10,11... | collective-permute-start | bytes 3538952 | tf_op jit(solution)/shard_map/ppermute | solution.py:596
  68.7 5.1 collective-permute-start.13
  107.6 12.5 %collective-permute-done.22 = bf16[64,640]{1,0:T(8,128)(2,1)S(1)} collective-permute-done((bf16[64,640]{1,0:T(8,128)(2,1)S(1)}, bf16[64,640]{1,0:T(8,128)(2,1)S(1)}, u32[]{:S(2)}, u32[]{:S(2)}) %collective-permute-start.22) | collective-permute-done | bytes 81952 | tf_op jit(solution)/shard_map/ppermute | solution.py:605
  127.3 13.4 %collective-permute-done.17 = bf16[4,64,640]{2,1,0:T(8,128)(2,1)S(1)} collective-permute-done((bf16[4,64,640]{2,1,0:T(8,128)(2,1)S(1)}, bf16[4,64,640]{2,1,0:T(8,128)(2,1)S(1)}, u32[]{:S(2)}, u32[]{:S(2)}) %collective-permute-start.17) | collective-permute-done | bytes 327712 | tf_op jit(solution)/shard_map/ppermute | solution.py:605
  144.2 6.3 collective-permute-done.23
  170.5 10.3 %shard_map.139 = (bf16[128,1024]{1,0:T(8,128)(2,1)S(1)}, f32[128,1024]{1,0:T(8,128)S(1)}, bf16[128,1024]{1,0:T(8,128)(2,1)S(1)}, f32[128,2560]{1,0:T(8,128)S(1)}...) custom-call(f32[128,1024]{1,0:T(8,128)S(1)} %copy.89.stream_ref, ...), custom_call_target="tpu_custom_call" | custom-call | flops 2359296000 | bytes 18874368 | tf_op jit(solution)/shard_map/pallas_call | solution.py:347
  181.9 4.8 shard_map.140
  186.7 5.2 collective-permute-start.30
  199.1 7.2 %collective-permute-start.33 = (bf16[4,64,640]{2,1,0:T(8,128)(2,1)S(1)}, bf16[4,64,640]{2,1,0:T(8,128)(2,1)S(1)}, u32[]{:S(2)}, u32[]{:S(2)}) collective-permute-start(bf16[4,64,640]{2,1,0:T(8,128)(2,1)S(1)} %get-tuple-element.162), channel_id=1, source_target_pairs={{0,24},{1,25},{2,26},{3,27},{4,28},{5,29},{6,30},{7,31},{8,0},{9,1... | collective-permute-start | bytes 983048 | tf_op jit(solution)/shard_map/ppermute | solution.py:605
  211.7 11.4 %collective-permute-done.36 = bf16[64,640]{1,0:T(8,128)(2,1)S(1)} collective-permute-done((bf16[64,640]{1,0:T(8,128)(2,1)S(1)}, bf16[64,640]{1,0:T(8,128)(2,1)S(1)}, u32[]{:S(2)}, u32[]{:S(2)}) %collective-permute-start.36) | collective-permute-done | bytes 81952 | tf_op jit(solution)/shard_map/ppermute | solution.py:605
  224.7 8.2 %collective-permute-done.31 = bf16[4,64,640]{2,1,0:T(8,128)(2,1)S(1)} collective-permute-done((bf16[4,64,640]{2,1,0:T(8,128)(2,1)S(1)}, bf16[4,64,640]{2,1,0:T(8,128)(2,1)S(1)}, u32[]{:S(2)}, u32[]{:S(2)}) %collective-permute-start.31) | collective-permute-done | bytes 327712 | tf_op jit(solution)/shard_map/ppermute | solution.py:605
  236.4 5.1 collective-permute-done.37
  255.0 10.4 %shard_map.143 = (bf16[128,1024]{1,0:T(8,128)(2,1)S(1)}, f32[128,1024]{1,0:T(8,128)S(1)}, bf16[128,1024]{1,0:T(8,128)(2,1)S(1)}, f32[128,2560]{1,0:T(8,128)S(1)}...) custom-call(f32[128,1024]{1,0:T(8,128)S(1)} %get-tuple-element.60.stream_ref, ...), custom_call_target="tpu_custom_call" | custom-call | flops 2359296000 | bytes 18874368 | tf_op jit(solution)/shard_map/pallas_call | solution.py:347
  266.2 9.2 %shard_map.144 = (bf16[128,1024]{1,0:T(8,128)(2,1)S(1)}, bf16[2,128,2560]{2,1,0:T(8,128)(2,1)S(1)}, f32[128,1024]{1,0:T(8,128)S(1)}, bf16[128,1024]{1,0:T(8,128)...) custom-call(f32[128,1024]{1,0:T(8,128)S(1)} %copy-done.8, ...), custom_call_target="tpu_custom_call" | custom-call | flops 2359296000 | bytes 18874368 | tf_op jit(solution)/shard_map/pallas_call | solution.py:421
  276.8 9.6 %shard_map.151 = bf16[32,4,544,128]{3,2,1,0:T(8,128)(2,1)} custom-call(bf16[2,128,2560]{2,1,0:T(8,128)(2,1)S(1)} %get-tuple-element.91.refs_0_, bf16[128,1024]{1,0:T(8,128)(2,1)S(1)} %get-tuple-element.92.refs_1_, bf16[128,1024]{1,0:T(8,128)(2,1)S(1)} %get-tuple-element.93.refs_2_, bf16[128,2560]{1,0:T(8,128)(2,1)S(1)} %get-tuple-element.94.refs_3_, ...), custom_call_target="tpu_custom_call" | custom-call | flops 2883584000 | bytes 20971520 | tf_op jit(solution)/shard_map/pallas_call | solution.py:490
  298.7 5.2 collective-permute-done.42
  310.6 5.2 collective-permute-start.51
  317.8 12.7 %collective-permute-start.45 = (bf16[4,64,640]{2,1,0:T(8,128)(2,1)S(1)}, bf16[4,64,640]{2,1,0:T(8,128)(2,1)S(1)}, u32[]{:S(2)}, u32[]{:S(2)}) collective-permute-start(bf16[4,64,640]{2,1,0:T(8,128)(2,1)S(1)} %get-tuple-element.137), channel_id=1, source_target_pairs={{0,24},{1,25},{2,26},{3,27},{4,28},{5,29},{6,30},{7,31},{8,0},{9,1... | collective-permute-start | bytes 983048 | tf_op jit(solution)/shard_map/ppermute | solution.py:605
  335.3 12.7 %collective-permute-start.54 = (bf16[64,640]{1,0:T(8,128)(2,1)S(1)}, bf16[64,640]{1,0:T(8,128)(2,1)S(1)}, u32[]{:S(2)}, u32[]{:S(2)}) collective-permute-start(bf16[64,640]{1,0:T(8,128)(2,1)S(1)} %get-tuple-element.157), channel_id=1, source_target_pairs={{0,24},{1,25},{2,26},{3,27},{4,28},{5,29},{6,30},{7,31},{8,0},{9,1... | collective-permute-start | bytes 245768 | tf_op jit(solution)/shard_map/ppermute | solution.py:605
  364.5 9.4 %shard_map.147 = (bf16[128,1024]{1,0:T(8,128)(2,1)S(1)}, bf16[2,128,2560]{2,1,0:T(8,128)(2,1)S(1)}, f32[128,1024]{1,0:T(8,128)S(1)}, bf16[128,1024]{1,0:T(8,128)...) custom-call(f32[128,1024]{1,0:T(8,128)S(1)} %get-tuple-element.75.grad_ref, ...), custom_call_target="tpu_custom_call" | custom-call | flops 2359296000 | bytes 18874368 | tf_op jit(solution)/shard_map/pallas_call | solution.py:421
  374.6 11.0 %shard_map.152 = bf16[32,4,672,128]{3,2,1,0:T(8,128)(2,1)} custom-call(bf16[2,128,2560]{2,1,0:T(8,128)(2,1)S(1)} %get-tuple-element.98.refs_0_, bf16[128,1024]{1,0:T(8,128)(2,1)S(1)} %copy-done.29, bf16[128,1024]{1,0:T(8,128)(2,1)S(1)} %get-tuple-element.100.refs_2_, bf16[128,2560]{1,0:T(8,128)(2,1)S(1)} %copy-done.17, ...), custom_call_target="tpu_custom_call" | custom-call | flops 2883584000 | bytes 20971520 | tf_op jit(solution)/shard_map/pallas_call | solution.py:490
  401.8 4.8 collective-permute-done.55
  418.3 5.3 collective-permute-start.58
  427.0 13.2 %collective-permute-done.62 = bf16[4,64,640]{2,1,0:T(8,128)(2,1)} collective-permute-done((bf16[4,64,640]{2,1,0:T(8,128)(2,1)}, bf16[4,64,640]{2,1,0:T(8,128)(2,1)}, u32[]{:S(2)}, u32[]{:S(2)}) %collective-permute-start.62) | collective-permute-done | bytes 327712 | tf_op jit(solution)/shard_map/ppermute | solution.py:601
  441.7 7.2 %collective-permute-start.67 = (bf16[64,640]{1,0:T(8,128)(2,1)S(1)}, bf16[64,640]{1,0:T(8,128)(2,1)S(1)}, u32[]{:S(2)}, u32[]{:S(2)}) collective-permute-start(bf16[64,640]{1,0:T(8,128)(2,1)S(1)} %get-tuple-element.151), channel_id=1, source_target_pairs={{0,24},{1,25},{2,26},{3,27},{4,28},{5,29},{6,30},{7,31},{8,0},{9,1... | collective-permute-start | bytes 245768 | tf_op jit(solution)/shard_map/ppermute | solution.py:605
  459.5 48.7 %collective-permute-start.69 = (bf16[544,128]{1,0:T(8,128)(2,1)S(1)}, bf16[544,128]{1,0:T(8,128)(2,1)S(1)}, u32[]{:S(2)}, u32[]{:S(2)}) collective-permute-start(bf16[544,128]{1,0:T(8,128)(2,1)S(1)} %get-tuple-element.146), channel_id=1, source_target_pairs={{0,64},{32,96},{64,0},{96,32},{1,65},{33,97},{65,1},{97,33},{2,66}... | collective-permute-start | bytes 417800 | tf_op jit(solution)/shard_map/ppermute | solution.py:687
  514.9 6.3 collective-permute-start.71
  534.0 49.3 %all-to-all-done = bf16[16,4,144,128]{3,2,1,0:T(8,128)(2,1)} async-done(((bf16[16,4,144,128]{3,2,1,0:T(8,128)(2,1)}), bf16[16,4,144,128]{3,2,1,0:T(8,128)(2,1)}, u32[]{:S(2)}, u32[]{:S(2)}) %all-to-all-start) | async-done | bytes 2359328 | tf_op jit(solution)/shard_map/all_to_all | solution.py:652
  592.7 15.9 %reduce-scatter.5.cloned.1.call-done = bf16[1,4,672,128]{3,2,1,0:T(8,128)(2,1)} async-done(((bf16[32,4,672,128]{3,2,1,0:T(8,128)(2,1)}), bf16[1,4,672,128]{3,2,1,0:T(8,128)(2,1)}) %reduce-scatter.5.cloned.1.call-update) | async-done | bytes 688144 | tf_op jit(solution)/shard_map/reduce_scatter | solution.py:796
  618.1 5.2 collective-permute-done.75
  (442 shorter events, 252.4 us)
Async XLA Ops:
  7.2 162.3 %all-gather.4.cloned.1.call-start = ((), (), s32[]{:S(2)}) async-start(), calls=%async_computation.5 | async-start | bytes 40157184 | tf_op jit(solution)/shard_map/all_gather | solution.py:726
  11.5 446.9 %reduce-scatter.3.cloned.1.call-start = ((), (), s32[]{:S(2)}) async-start(), calls=%async_computation.3 | async-start | bytes 18382848 | tf_op jit(solution)/shard_map/reduce_scatter | solution.py:796
  41.6 27.0 %collective-permute-start.11 = (bf16[4,2,144,128]{3,2,1,0:T(8,128)(2,1)S(1)}, bf16[4,2,144,128]{3,2,1,0:T(8,128)(2,1)S(1)}, u32[]{:S(2)}, u32[]{:S(2)}) collective-permute-start(bf16[4,2,144,128]{3,2,1,0:T(8,128)(2,1)S(1)} %get-tuple-element.168), channel_id=1, source_target_pairs={{0,6},{1,7},{2,0},{3,1},{4,2},{5,3},{6,4},{7,5},{8,14},{9,15},{10,... | collective-permute-start | bytes 884744 | tf_op jit(solution)/shard_map/ppermute | solution.py:601
  43.9 24.6 %collective-permute-start.10 = (bf16[4,2,144,128]{3,2,1,0:T(8,128)(2,1)S(1)}, bf16[4,2,144,128]{3,2,1,0:T(8,128)(2,1)S(1)}, u32[]{:S(2)}, u32[]{:S(2)}) collective-permute-start(bf16[4,2,144,128]{3,2,1,0:T(8,128)(2,1)S(1)} %get-tuple-element.168), channel_id=1, source_target_pairs={{0,4},{1,5},{2,6},{3,7},{4,0},{5,1},{6,2},{7,3},{8,12},{9,13},{10,... | collective-permute-start | bytes 884744 | tf_op jit(solution)/shard_map/ppermute | solution.py:601
  44.6 24.0 %collective-permute-start.9 = (bf16[4,2,144,128]{3,2,1,0:T(8,128)(2,1)S(1)}, bf16[4,2,144,128]{3,2,1,0:T(8,128)(2,1)S(1)}, u32[]{:S(2)}, u32[]{:S(2)}) collective-permute-start(bf16[4,2,144,128]{3,2,1,0:T(8,128)(2,1)S(1)} %get-tuple-element.168), channel_id=1, source_target_pairs={{0,2},{1,3},{2,4},{3,5},{4,6},{5,7},{6,0},{7,1},{8,10},{9,11},{10,... | collective-permute-start | bytes 884744 | tf_op jit(solution)/shard_map/ppermute | solution.py:601
  52.2 22.1 %collective-permute-start.12 = (bf16[4,4,2,144,128]{4,3,2,1,0:T(8,128)(2,1)S(1)}, bf16[4,4,2,144,128]{4,3,2,1,0:T(8,128)(2,1)}, u32[]{:S(2)}, u32[]{:S(2)}) collective-permute-start(bf16[4,4,2,144,128]{4,3,2,1,0:T(8,128)(2,1)S(1)} %pad_maximum_fusion.4.first_own), channel_id=1, source_target_pairs={{0,1},{1,0},{2,3},{3,2},{4,5},{5,4},{6,7},{7,6},{8,9},{9,8},{10,11... | collective-permute-start | bytes 3538952 | tf_op jit(solution)/shard_map/ppermute | solution.py:596
  99.0 24.4 %collective-permute-start.19 = (bf16[4,64,640]{2,1,0:T(8,128)(2,1)S(1)}, bf16[4,64,640]{2,1,0:T(8,128)(2,1)S(1)}, u32[]{:S(2)}, u32[]{:S(2)}) collective-permute-start(bf16[4,64,640]{2,1,0:T(8,128)(2,1)S(1)} %get-tuple-element.166), channel_id=1, source_target_pairs={{0,24},{1,25},{2,26},{3,27},{4,28},{5,29},{6,30},{7,31},{8,0},{9,1... | collective-permute-start | bytes 983048 | tf_op jit(solution)/shard_map/ppermute | solution.py:605
  102.6 17.5 %collective-permute-start.22 = (bf16[64,640]{1,0:T(8,128)(2,1)S(1)}, bf16[64,640]{1,0:T(8,128)(2,1)S(1)}, u32[]{:S(2)}, u32[]{:S(2)}) collective-permute-start(bf16[64,640]{1,0:T(8,128)(2,1)S(1)} %get-tuple-element.179), channel_id=1, source_target_pairs={{0,24},{1,25},{2,26},{3,27},{4,28},{5,29},{6,30},{7,31},{8,0},{9,1... | collective-permute-start | bytes 245768 | tf_op jit(solution)/shard_map/ppermute | solution.py:605
  102.6 18.1 %collective-permute-start.21 = (bf16[64,640]{1,0:T(8,128)(2,1)S(1)}, bf16[64,640]{1,0:T(8,128)(2,1)S(1)}, u32[]{:S(2)}, u32[]{:S(2)}) collective-permute-start(bf16[64,640]{1,0:T(8,128)(2,1)S(1)} %get-tuple-element.179), channel_id=1, source_target_pairs={{0,16},{1,17},{2,18},{3,19},{4,20},{5,21},{6,22},{7,23},{8,24},{9,... | collective-permute-start | bytes 245768 | tf_op jit(solution)/shard_map/ppermute | solution.py:605
  102.8 18.0 %collective-permute-start.20 = (bf16[64,640]{1,0:T(8,128)(2,1)S(1)}, bf16[64,640]{1,0:T(8,128)(2,1)S(1)}, u32[]{:S(2)}, u32[]{:S(2)}) collective-permute-start(bf16[64,640]{1,0:T(8,128)(2,1)S(1)} %get-tuple-element.179), channel_id=1, source_target_pairs={{0,8},{1,9},{2,10},{3,11},{4,12},{5,13},{6,14},{7,15},{8,16},{9,17... | collective-permute-start | bytes 245768 | tf_op jit(solution)/shard_map/ppermute | solution.py:605
  104.0 23.3 %collective-permute-start.18 = (bf16[4,64,640]{2,1,0:T(8,128)(2,1)S(1)}, bf16[4,64,640]{2,1,0:T(8,128)(2,1)S(1)}, u32[]{:S(2)}, u32[]{:S(2)}) collective-permute-start(bf16[4,64,640]{2,1,0:T(8,128)(2,1)S(1)} %get-tuple-element.166), channel_id=1, source_target_pairs={{0,16},{1,17},{2,18},{3,19},{4,20},{5,21},{6,22},{7,23},{8,24},{9,... | collective-permute-start | bytes 983048 | tf_op jit(solution)/shard_map/ppermute | solution.py:605
  120.1 20.7 %collective-permute-start.17 = (bf16[4,64,640]{2,1,0:T(8,128)(2,1)S(1)}, bf16[4,64,640]{2,1,0:T(8,128)(2,1)S(1)}, u32[]{:S(2)}, u32[]{:S(2)}) collective-permute-start(bf16[4,64,640]{2,1,0:T(8,128)(2,1)S(1)} %get-tuple-element.166), channel_id=1, source_target_pairs={{0,8},{1,9},{2,10},{3,11},{4,12},{5,13},{6,14},{7,15},{8,16},{9,17... | collective-permute-start | bytes 983048 | tf_op jit(solution)/shard_map/ppermute | solution.py:605
  120.9 23.4 %collective-permute-start.25 = (bf16[4,64,640]{2,1,0:T(8,128)(2,1)S(1)}, bf16[4,64,640]{2,1,0:T(8,128)(2,1)S(1)}, u32[]{:S(2)}, u32[]{:S(2)}) collective-permute-start(bf16[4,64,640]{2,1,0:T(8,128)(2,1)S(1)} %get-tuple-element.164), channel_id=1, source_target_pairs={{0,6},{1,7},{2,0},{3,1},{4,2},{5,3},{6,4},{7,5},{8,14},{9,15},{10,... | collective-permute-start | bytes 983048 | tf_op jit(solution)/shard_map/ppermute | solution.py:601
  122.3 21.9 %collective-permute-start.24 = (bf16[4,64,640]{2,1,0:T(8,128)(2,1)S(1)}, bf16[4,64,640]{2,1,0:T(8,128)(2,1)S(1)}, u32[]{:S(2)}, u32[]{:S(2)}) collective-permute-start(bf16[4,64,640]{2,1,0:T(8,128)(2,1)S(1)} %get-tuple-element.164), channel_id=1, source_target_pairs={{0,4},{1,5},{2,6},{3,7},{4,0},{5,1},{6,2},{7,3},{8,12},{9,13},{10,... | collective-permute-start | bytes 983048 | tf_op jit(solution)/shard_map/ppermute | solution.py:601
  123.4 27.1 %collective-permute-start.23 = (bf16[4,64,640]{2,1,0:T(8,128)(2,1)S(1)}, bf16[4,64,640]{2,1,0:T(8,128)(2,1)S(1)}, u32[]{:S(2)}, u32[]{:S(2)}) collective-permute-start(bf16[4,64,640]{2,1,0:T(8,128)(2,1)S(1)} %get-tuple-element.164), channel_id=1, source_target_pairs={{0,2},{1,3},{2,4},{3,5},{4,6},{5,7},{6,0},{7,1},{8,10},{9,11},{10,... | collective-permute-start | bytes 983048 | tf_op jit(solution)/shard_map/ppermute | solution.py:601
  142.0 18.3 %collective-permute-start.26 = (bf16[4,4,64,640]{3,2,1,0:T(8,128)(2,1)}, bf16[4,4,64,640]{3,2,1,0:T(8,128)(2,1)}, u32[]{:S(2)}, u32[]{:S(2)}) collective-permute-start(bf16[4,4,64,640]{3,2,1,0:T(8,128)(2,1)} %pad_maximum_fusion.first_own), channel_id=1, source_target_pairs={{0,1},{1,0},{2,3},{3,2},{4,5},{5,4},{6,7},{7,6},{8,9},{9,8},{10,11... | collective-permute-start | bytes 3932168 | tf_op jit(solution)/shard_map/ppermute | solution.py:596
  199.1 24.5 %collective-permute-start.33 = (bf16[4,64,640]{2,1,0:T(8,128)(2,1)S(1)}, bf16[4,64,640]{2,1,0:T(8,128)(2,1)S(1)}, u32[]{:S(2)}, u32[]{:S(2)}) collective-permute-start(bf16[4,64,640]{2,1,0:T(8,128)(2,1)S(1)} %get-tuple-element.162), channel_id=1, source_target_pairs={{0,24},{1,25},{2,26},{3,27},{4,28},{5,29},{6,30},{7,31},{8,0},{9,1... | collective-permute-start | bytes 983048 | tf_op jit(solution)/shard_map/ppermute | solution.py:605
  223.6 17.9 %collective-permute-start.37 = (bf16[4,64,640]{2,1,0:T(8,128)(2,1)S(1)}, bf16[4,64,640]{2,1,0:T(8,128)(2,1)S(1)}, u32[]{:S(2)}, u32[]{:S(2)}) collective-permute-start(bf16[4,64,640]{2,1,0:T(8,128)(2,1)S(1)} %get-tuple-element.160), channel_id=1, source_target_pairs={{0,2},{1,3},{2,4},{3,5},{4,6},{5,7},{6,0},{7,1},{8,10},{9,11},{10,... | collective-permute-start | bytes 983048 | tf_op jit(solution)/shard_map/ppermute | solution.py:601
  286.5 322.1 %reduce-scatter.5.cloned.1.call-start = ((), (), s32[]{:S(2)}) async-start(), calls=%async_computation.4 | async-start | bytes 22708224 | tf_op jit(solution)/shard_map/reduce_scatter | solution.py:796
  310.6 19.9 %collective-permute-start.51 = (bf16[4,64,640]{2,1,0:T(8,128)(2,1)}, bf16[4,64,640]{2,1,0:T(8,128)(2,1)}, u32[]{:S(2)}, u32[]{:S(2)}) collective-permute-start(bf16[4,64,640]{2,1,0:T(8,128)(2,1)} %get-tuple-element.140), channel_id=1, source_target_pairs={{0,6},{1,7},{2,0},{3,1},{4,2},{5,3},{6,4},{7,5},{8,14},{9,15},{10,... | collective-permute-start | bytes 983048 | tf_op jit(solution)/shard_map/ppermute | solution.py:601
  315.8 17.9 %collective-permute-start.49 = (bf16[4,64,640]{2,1,0:T(8,128)(2,1)}, bf16[4,64,640]{2,1,0:T(8,128)(2,1)}, u32[]{:S(2)}, u32[]{:S(2)}) collective-permute-start(bf16[4,64,640]{2,1,0:T(8,128)(2,1)} %get-tuple-element.138), channel_id=1, source_target_pairs={{0,2},{1,3},{2,4},{3,5},{4,6},{5,7},{6,0},{7,1},{8,10},{9,11},{10,... | collective-permute-start | bytes 983048 | tf_op jit(solution)/shard_map/ppermute | solution.py:601
  317.8 30.3 %collective-permute-start.45 = (bf16[4,64,640]{2,1,0:T(8,128)(2,1)S(1)}, bf16[4,64,640]{2,1,0:T(8,128)(2,1)S(1)}, u32[]{:S(2)}, u32[]{:S(2)}) collective-permute-start(bf16[4,64,640]{2,1,0:T(8,128)(2,1)S(1)} %get-tuple-element.137), channel_id=1, source_target_pairs={{0,24},{1,25},{2,26},{3,27},{4,28},{5,29},{6,30},{7,31},{8,0},{9,1... | collective-permute-start | bytes 983048 | tf_op jit(solution)/shard_map/ppermute | solution.py:605
  330.5 18.2 %collective-permute-start.44 = (bf16[4,64,640]{2,1,0:T(8,128)(2,1)S(1)}, bf16[4,64,640]{2,1,0:T(8,128)(2,1)S(1)}, u32[]{:S(2)}, u32[]{:S(2)}) collective-permute-start(bf16[4,64,640]{2,1,0:T(8,128)(2,1)S(1)} %get-tuple-element.136), channel_id=1, source_target_pairs={{0,16},{1,17},{2,18},{3,19},{4,20},{5,21},{6,22},{7,23},{8,24},{9,... | collective-permute-start | bytes 983048 | tf_op jit(solution)/shard_map/ppermute | solution.py:605
  330.5 19.4 %collective-permute-start.43 = (bf16[4,64,640]{2,1,0:T(8,128)(2,1)S(1)}, bf16[4,64,640]{2,1,0:T(8,128)(2,1)S(1)}, u32[]{:S(2)}, u32[]{:S(2)}) collective-permute-start(bf16[4,64,640]{2,1,0:T(8,128)(2,1)S(1)} %get-tuple-element.135), channel_id=1, source_target_pairs={{0,8},{1,9},{2,10},{3,11},{4,12},{5,13},{6,14},{7,15},{8,16},{9,17... | collective-permute-start | bytes 983048 | tf_op jit(solution)/shard_map/ppermute | solution.py:605
  335.3 19.2 %collective-permute-start.54 = (bf16[64,640]{1,0:T(8,128)(2,1)S(1)}, bf16[64,640]{1,0:T(8,128)(2,1)S(1)}, u32[]{:S(2)}, u32[]{:S(2)}) collective-permute-start(bf16[64,640]{1,0:T(8,128)(2,1)S(1)} %get-tuple-element.157), channel_id=1, source_target_pairs={{0,24},{1,25},{2,26},{3,27},{4,28},{5,29},{6,30},{7,31},{8,0},{9,1... | collective-permute-start | bytes 245768 | tf_op jit(solution)/shard_map/ppermute | solution.py:605
  417.2 23.0 %collective-permute-start.62 = (bf16[4,64,640]{2,1,0:T(8,128)(2,1)}, bf16[4,64,640]{2,1,0:T(8,128)(2,1)}, u32[]{:S(2)}, u32[]{:S(2)}) collective-permute-start(bf16[4,64,640]{2,1,0:T(8,128)(2,1)} %get-tuple-element.132), channel_id=1, source_target_pairs={{0,2},{1,3},{2,4},{3,5},{4,6},{5,7},{6,0},{7,1},{8,10},{9,11},{10,... | collective-permute-start | bytes 983048 | tf_op jit(solution)/shard_map/ppermute | solution.py:601
  418.3 30.6 %collective-permute-start.58 = (bf16[4,64,640]{2,1,0:T(8,128)(2,1)S(1)}, bf16[4,64,640]{2,1,0:T(8,128)(2,1)S(1)}, u32[]{:S(2)}, u32[]{:S(2)}) collective-permute-start(bf16[4,64,640]{2,1,0:T(8,128)(2,1)S(1)} %get-tuple-element.131), channel_id=1, source_target_pairs={{0,24},{1,25},{2,26},{3,27},{4,28},{5,29},{6,30},{7,31},{8,0},{9,1... | collective-permute-start | bytes 983048 | tf_op jit(solution)/shard_map/ppermute | solution.py:605
  423.7 26.1 %collective-permute-start.57 = (bf16[4,64,640]{2,1,0:T(8,128)(2,1)S(1)}, bf16[4,64,640]{2,1,0:T(8,128)(2,1)S(1)}, u32[]{:S(2)}, u32[]{:S(2)}) collective-permute-start(bf16[4,64,640]{2,1,0:T(8,128)(2,1)S(1)} %get-tuple-element.130), channel_id=1, source_target_pairs={{0,16},{1,17},{2,18},{3,19},{4,20},{5,21},{6,22},{7,23},{8,24},{9,... | collective-permute-start | bytes 983048 | tf_op jit(solution)/shard_map/ppermute | solution.py:605
  426.0 23.8 %collective-permute-start.56 = (bf16[4,64,640]{2,1,0:T(8,128)(2,1)S(1)}, bf16[4,64,640]{2,1,0:T(8,128)(2,1)S(1)}, u32[]{:S(2)}, u32[]{:S(2)}) collective-permute-start(bf16[4,64,640]{2,1,0:T(8,128)(2,1)S(1)} %get-tuple-element.129), channel_id=1, source_target_pairs={{0,8},{1,9},{2,10},{3,11},{4,12},{5,13},{6,14},{7,15},{8,16},{9,17... | collective-permute-start | bytes 983048 | tf_op jit(solution)/shard_map/ppermute | solution.py:605
  459.4 51.6 %collective-permute-start.70 = (bf16[544,128]{1,0:T(8,128)(2,1)S(1)}, bf16[544,128]{1,0:T(8,128)(2,1)S(1)}, u32[]{:S(2)}, u32[]{:S(2)}) collective-permute-start(bf16[544,128]{1,0:T(8,128)(2,1)S(1)} %get-tuple-element.145), channel_id=1, source_target_pairs={{0,96},{32,0},{64,32},{96,64},{1,97},{33,1},{65,33},{97,65},{2,98}... | collective-permute-start | bytes 417800 | tf_op jit(solution)/shard_map/ppermute | solution.py:687
  459.5 51.5 %collective-permute-start.69 = (bf16[544,128]{1,0:T(8,128)(2,1)S(1)}, bf16[544,128]{1,0:T(8,128)(2,1)S(1)}, u32[]{:S(2)}, u32[]{:S(2)}) collective-permute-start(bf16[544,128]{1,0:T(8,128)(2,1)S(1)} %get-tuple-element.146), channel_id=1, source_target_pairs={{0,64},{32,96},{64,0},{96,32},{1,65},{33,97},{65,1},{97,33},{2,66}... | collective-permute-start | bytes 417800 | tf_op jit(solution)/shard_map/ppermute | solution.py:687
  527.4 55.9 %all-to-all-start = ((bf16[16,4,144,128]{3,2,1,0:T(8,128)(2,1)}), bf16[16,4,144,128]{3,2,1,0:T(8,128)(2,1)}, u32[]{:S(2)}, u32[]{:S(2)}) async-start(bf16[16,4,144,128]{3,2,1,0:T(8,128)(2,1)} %fusion.2), calls=%async_computation.1 | async-start | bytes 4718592 | tf_op jit(solution)/shard_map/all_to_all | solution.py:652
  (107 other events, 977.0 us)
Sparse Core Ops, SparseCore 0:
  11.6 150.4 all-gather.3
  286.6 162.3 reduce-scatter.2
  453.5 155.0 reduce-scatter.4
